TPU v7x, 512 devices: a whole 4x4x16 slice. The times are simulated.
512 devices in a mesh: dp: 32 (over x, y, core), mp: 16 (over z).
Axes of the slice: x: 4, y: 4, z: 16, core: 2. Of those that a mesh axis runs over, the one named last changes fastest.
Arguments:
- grads: bfloat16 [32, 1024, 10240], P('dp', None, 'mp'), may hold values from -4 to 4
- left_factor: float32 [16, 3, 1024, 1024], P('mp', None, 'dp'), may hold values from -0.3 to 0.3
- left_root: bfloat16 [16, 3, 1024, 1024], P('mp', None, 'dp'), may hold values from -2.5 to 2.5
- right_q: float32 [16, 512, 512], P('mp', 'dp'), may hold values from -0.3 to 0.3
- right_kv: float32 [16, 2, 64, 64], P('mp'), may hold values from -0.3 to 0.3
- right_q_root: bfloat16 [16, 512, 512], P('mp'), may hold values from -2.5 to 2.5
- right_kv_root: bfloat16 [16, 2, 64, 64], P('mp'), may hold values from -2.5 to 2.5
- moment: float32 [1024, 10240], P('dp', 'mp'), may hold values from 0.001 to 0.1
Outputs:
- direction: bfloat16 [1024, 10240], P(None, 'mp')
- left_new: float32 [16, 3, 1024, 1024], P('mp', None, 'dp')
- right_q_new: float32 [16, 512, 512], P('mp', 'dp')
- right_kv_new: float32 [16, 2, 64, 64], P('mp')
- moment_new: float32 [1024, 10240], P('dp', 'mp')
All inputs are finite; a program needn't handle non-finite values.
Results may differ from a plain program's by a relative error of at most 0.024.
Values may be sent and summed in bfloat16 or wider, within the bound.
A program may use at most 64 MiB of HBM per device.

v0:
```python
import jax
import jax.numpy as jnp
from jax import lax
from jax.sharding import PartitionSpec as P

factor_keep = 0.95
factor_add = 0.05
moment_keep = 0.99
moment_add = 0.01
graft_eps = 1e-08
norm_eps = 1e-06


def block_spans(q_cols, kv_cols):
    return ((0, q_cols), (q_cols, kv_cols), (q_cols + kv_cols, kv_cols))


def row_product(first, second):
    return lax.dot_general(
        first, second, (((1,), (1,)), ((), ())), preferred_element_type=jnp.float32
    )


def column_product(first, second):
    return lax.dot_general(
        first, second, (((0,), (0,)), ((), ())), preferred_element_type=jnp.float32
    )


def local(grads, left_factor, left_root, right_q, right_kv, right_q_root, right_kv_root, moment):
    replicas = lax.axis_size("dp")
    my_index = lax.axis_index("dp")
    order = left_factor.shape[3]
    panel = order // replicas
    q_cols = right_q_root.shape[1]
    kv_cols = right_kv.shape[2]
    q_panel = right_q.shape[1]
    spans = block_spans(q_cols, kv_cols)
    summed = lax.psum(grads[0].astype(jnp.float32).astype(jnp.bfloat16), "dp")
    my_rows = lax.dynamic_slice_in_dim(summed, my_index * panel, panel, 0)
    row_grad = my_rows.astype(jnp.float32)
    moment_new = moment_keep * moment + moment_add * row_grad * row_grad
    graft = row_grad / (jnp.sqrt(moment_new) + graft_eps)
    graft_terms = jnp.stack(
        [jnp.sum(jnp.square(graft[:, offset : offset + extent])) for offset, extent in spans]
    )
    left_list = []
    precond_list = []
    kv_list = []
    for number in range(3):
        offset, extent = spans[number]
        block_grad = summed[:, offset : offset + extent]
        owned = my_rows[:, offset : offset + extent]
        left_list.append(
            factor_keep * left_factor[0, number] + factor_add * row_product(owned, block_grad)
        )
        projected = jnp.dot(
            left_root[0, number], block_grad, preferred_element_type=jnp.float32
        ).astype(jnp.bfloat16)
        if number == 0:
            root_block = right_q_root[0]
        else:
            root_block = right_kv_root[0, number - 1]
            kv_list.append(
                factor_keep * right_kv[0, number - 1]
                + factor_add * column_product(block_grad, block_grad)
            )
        precond_list.append(jnp.dot(projected, root_block, preferred_element_type=jnp.float32))
    query_grad = summed[:, :q_cols]
    query_slice = lax.dynamic_slice_in_dim(query_grad, my_index * q_panel, q_panel, 1)
    right_q_new = factor_keep * right_q[0] + factor_add * column_product(query_slice, query_grad)
    shampoo_terms = jnp.stack([jnp.sum(jnp.square(precond)) for precond in precond_list])
    graft_sq, shampoo_sq = lax.psum((graft_terms, shampoo_terms), ("dp", "mp"))
    scale = jnp.sqrt(graft_sq / (shampoo_sq + norm_eps))
    rows_out = jnp.concatenate(
        [scale[number] * precond_list[number] for number in range(3)], axis=1
    ).astype(jnp.bfloat16)
    direction = lax.all_gather(rows_out, "dp", axis=0, tiled=True)
    return (
        direction,
        jnp.stack(left_list)[None],
        right_q_new[None],
        jnp.stack(kv_list)[None],
        moment_new,
    )


def solution(mesh):
    return jax.shard_map(
        local,
        mesh=mesh,
        in_specs=(
            P("dp", None, "mp"),
            P("mp", None, "dp", None),
            P("mp", None, "dp", None),
            P("mp", "dp", None),
            P("mp", None, None, None),
            P("mp", None, None),
            P("mp", None, None, None),
            P("dp", "mp"),
        ),
        out_specs=(
            P(None, "mp"),
            P("mp", None, "dp", None),
            P("mp", "dp", None),
            P("mp", None, None, None),
            P("dp", "mp"),
        ),
        check_vma=False,
    )
```

profile of v0, /device:TPU:1, one launch (start us, length us, event | category | flops | bytes accessed | tf_op | source)
XLA Modules:
  0.0 336.3 jit_solution(918089584608072145)
XLA Ops:
  7.2 0.0 copy-start
  7.2 0.0 copy-start.3
  7.2 0.0 copy-start.5
  7.2 0.0 copy-start.7
  7.2 0.0 all-reduce.3.cloned.1.call-start
  7.3 0.7 all-reduce.3.cloned.1.call-update
  7.9 0.0 all-gather.2.cloned.1.call-start
  8.0 144.5 %all-reduce.3.cloned.1.call-done = bf16[1024,640]{1,0:T(8,128)(2,1)} async-done(((bf16[1024,640]{1,0:T(8,128)(2,1)}), bf16[1024,640]{1,0:T(8,128)(2,1)}) %all-reduce.3.cloned.1.call-update) | async-done | bytes 1310736 | tf_op jit(solution)/shard_map/psum | solution.py:39
  152.5 0.0 copy-done.3
  152.5 1.4 convert_divide_fusion
  154.0 0.6 fusion.26
  154.6 0.7 fusion.41
  155.2 0.0 copy-done.5
  155.2 0.0 copy-done.7
  155.2 1.9 multiply_reduce_fusion.1
  157.2 1.9 multiply_reduce_fusion.2
  159.0 0.0 copy-done
  159.0 2.4 multiply_reduce_fusion
  161.4 0.0 copy-start.1
  161.4 0.0 copy-start.6
  161.4 4.1 %pad_maximum_fusion.1 = (f32[3]{0:T(128)S(1)}, f32[3]{0:T(128)S(1)}) fusion(f32[1]{0:T(128)} %bitcast.3, f32[1]{0:T(128)} %bitcast.2, f32[1]{0:T(128)} %bitcast.1, f32[1]{0:T(128)} %bitcast.12, f32[1]{0:T(128)} %bitcast.9, f32[1]{0:T(128)} %bitcast.6), kind=kLoop, calls=%fused_computation.65 | loop fusion | flops 12 | bytes 48 | tf_op jit(solution)/shard_map/stack | solution.py:44
  165.5 105.0 %all-reduce = (f32[3]{0:T(128)S(1)}, f32[3]{0:T(128)S(1)}) all-reduce(f32[3]{0:T(128)S(1)} %get-tuple-element.20, f32[3]{0:T(128)S(1)} %get-tuple-element.21), channel_id=1, replica_groups=mesh['dp'=32,'mp'=16] {'dp','mp'}, use_global_device_ids=true, to_apply=%region_4.0 | all-reduce | flops 6 | bytes 48 | tf_op jit(solution)/shard_map/psum | solution.py:73
  270.5 0.6 fusion.55
  271.1 0.7 multiply_convert_fusion
  271.8 0.7 multiply_convert_fusion.1
  272.4 0.7 multiply_convert_fusion.2
  273.1 0.7 pad_maximum_fusion
  273.8 0.0 all-gather.2.cloned.1.call-update
  273.8 0.0 copy-start.2
  273.8 0.0 copy-done.1
  273.8 0.0 copy-done.6
  273.8 0.2 fusion.10
  274.1 0.4 fusion.8
  274.5 0.6 maximum_bitcast_fusion.1
  275.1 0.0 copy-done.2
  275.1 0.3 fusion.3
  275.4 0.0 slice-start
  275.4 0.0 copy-start.4
  275.4 0.2 fusion.5
  275.6 0.4 fusion.1
  276.1 0.8 maximum_bitcast_fusion
  276.8 0.0 slice-done
  276.8 0.0 copy-done.4
  276.8 1.0 fusion.12
  277.8 49.1 %all-gather.2.cloned.1.call-done = bf16[1024,640]{1,0:T(8,128)(2,1)} async-done(((bf16[32,640]{1,0:T(8,128)(2,1)}), bf16[1024,640]{1,0:T(8,128)(2,1)}) %all-gather.2.cloned.1.call-update) | async-done | bytes 1310736 | tf_op jit(solution)/shard_map/all_gather | solution.py:78
  327.0 2.5 copy.16
  (1 shorter events, 0.0 us)
Async XLA Ops:
  7.2 151.9 %copy-start = (bf16[1,512,512]{2,1,0:T(8,128)(2,1)S(1)}, bf16[1,512,512]{2,1,0:T(8,128)(2,1)}, u32[]{:S(2)}) copy-start(bf16[1,512,512]{2,1,0:T(8,128)(2,1)} %param.13) | copy-start | bytes 1572868
  7.2 145.3 %copy-start.3 = (f32[32,640]{1,0:T(8,128)S(1)}, f32[32,640]{1,0:T(8,128)}, u32[]{:S(2)}) copy-start(f32[32,640]{1,0:T(8,128)} %param.15) | copy-start | bytes 245764
  7.2 148.1 %copy-start.5 = (bf16[1,3,32,1024]{3,2,1,0:T(8,128)(2,1)S(1)}, bf16[1,3,32,1024]{3,2,1,0:T(8,128)(2,1)}, u32[]{:S(2)}) copy-start(bf16[1,3,32,1024]{3,2,1,0:T(8,128)(2,1)} %param.10) | copy-start | bytes 589828
  7.2 148.0 %copy-start.7 = (bf16[1,2,64,64]{3,2,1,0:T(8,128)(2,1)S(1)}, bf16[1,2,64,64]{3,2,1,0:T(8,128)(2,1)}, u32[]{:S(2)}) copy-start(bf16[1,2,64,64]{3,2,1,0:T(8,128)(2,1)} %param.14) | copy-start | bytes 49156
  7.2 145.3 %all-reduce.3.cloned.1.call-start = ((), (), s32[]{:S(2)}) async-start(), calls=%async_computation | async-start | bytes 2621440 | tf_op jit(solution)/shard_map/psum | solution.py:39
  7.9 319.0 %all-gather.2.cloned.1.call-start = ((), (), s32[]{:S(2)}) async-start(), calls=%async_computation.1 | async-start | bytes 1351680 | tf_op jit(solution)/shard_map/all_gather | solution.py:78
  161.4 112.4 %copy-start.1 = (bf16[1024,640]{1,0:T(8,128)(2,1)S(1)}, bf16[1024,640]{1,0:T(8,128)(2,1)}, u32[]{:S(2)}) copy-start(bf16[1024,640]{1,0:T(8,128)(2,1)} %all-reduce.3.cloned.1.call-done) | copy-start | bytes 3932164
  161.4 112.4 %copy-start.6 = (f32[1,2,64,64]{3,2,1,0:T(8,128)S(1)}, f32[1,2,64,64]{3,2,1,0:T(8,128)}, u32[]{:S(2)}) copy-start(f32[1,2,64,64]{3,2,1,0:T(8,128)} %param.12) | copy-start | bytes 98308
  273.8 1.3 copy-start.2
  275.4 1.4 slice-start
  275.4 1.4 copy-start.4
Sparse Core Ops, SparseCore 0:
  11.3 141.1 all-reduce.2
  273.9 52.9 all-gather.1
where the time goes:
time: 337 us; the launch traced here: 336 us
  waiting for transfers between devices  194 us (58%)
  blocking collectives  105 us (31%)
  between operations  14.2 us (4%)
  other arithmetic  10.9 us (3%)
  matrix products  8.68 us (3%)
    psum x1, waiting for transfers between devices, local(): summed = lax.psum(grads[0].astype(jnp.float32).astype(jnp.bfloat16), 'dp')  144 us
    psum x1, blocking collectives, local(): graft_sq, shampoo_sq = lax.psum((graft_terms, shampoo_terms), ('dp', 'mp'))  105 us
    all_gather x1, waiting for transfers between devices, local(): direction = lax.all_gather(rows_out, 'dp', axis=0, tiled=True)  49.1 us
  transfers between devices with their start and end apart: 2, of which 2 were waited for; matrix products, arithmetic and copies ran while one was open for 1% of the time, Pallas kernels for 0%

commit v1 on v0

v1 whole, which is shorter than its diff:
```python
import jax
import jax.numpy as jnp
from jax import lax
from jax.experimental import pallas as pl
from jax.experimental.pallas import tpu as pltpu
from jax.sharding import PartitionSpec as P

MESH = pl.DeviceIdType.MESH
f32 = jnp.float32
bf16 = jnp.bfloat16

factor_keep = 0.95
factor_add = 0.05
moment_keep = 0.99
moment_add = 0.01
graft_eps = 1e-08
norm_eps = 1e-06

SIDE = 4
HALF = 16
QC = 512
KC = 64
COLS = QC + 2 * KC
ORDER = 1024
PANEL = 32
FAR_FIRST = (2, 1, 3)


def dot(a, b, ca=1, cb=0):
    return lax.dot_general(a, b, (((ca,), (cb,)), ((), ())), preferred_element_type=f32)


def kernel(
    depth,
    g, lf, lr, rq, rkv, rqr, rkvr, mom,
    gathered, scale_row, left_new, rq_new, rkv_new, mom_new,
    own, sib, part, relayed, recv1, acc, part2, recv2, total,
    lf_v, lr_v, rq_v, rkv_v, rqr_v, rkvr_v, mom_v,
    diag, slab, norm, norm_in, norm_z,
    ssem, rsem, lsem,
):
    dp = lax.axis_index("dp")
    z = lax.axis_index("mp")
    core = lax.rem(dp, 2)
    other = 1 - core
    y = lax.rem(dp // 2, SIDE)
    x = dp // (2 * SIDE)

    def at(i, j, k):
        return ((i * SIDE + j) * 2 + k, z)

    sibling = at(x, y, other)
    xs = [x] + [lax.rem(x + k, SIDE) for k in range(1, SIDE)]
    ys = [y] + [lax.rem(y + k, SIDE) for k in range(1, SIDE)]
    on_x = [None] + [at(xs[k], y, core) for k in range(1, SIDE)]
    on_y = [None] + [at(x, ys[k], core) for k in range(1, SIDE)]
    first = (on_x, on_y)
    second = (on_y, on_x)
    on_z = [None] + [(dp, lax.rem(z + k, depth)) for k in range(1, depth)]

    started = []
    local = []

    def send(src, dst, device):
        i = len(started)
        copy = pltpu.make_async_remote_copy(
            src_ref=src, dst_ref=dst, send_sem=ssem.at[i], recv_sem=rsem.at[i],
            device_id=device, device_id_type=MESH,
        )
        copy.start()
        started.append(copy)
        return copy

    def load(src, dst):
        copy = pltpu.make_async_copy(src, dst, lsem.at[len(local)])
        copy.start()
        local.append(copy)
        return copy

    def group(ref, h, k, c):
        return ref.at[xs[k], :, c, 0] if h == 0 else ref.at[:, ys[k], c, 1]

    order0 = FAR_FIRST + (0,)
    mine = {(h, k): load(group(g, h, k, core), own.at[h, k]) for k in order0 for h in range(2)}

    barrier = pltpu.get_barrier_semaphore()
    partners = [sibling] + on_x[1:] + on_y[1:] + on_z[1:]
    for device in partners:
        pl.semaphore_signal(barrier, inc=1, device_id=device, device_id_type=MESH)
    pl.semaphore_wait(barrier, len(partners))

    pair = {(h, k): send(group(g, h, k, other), sib.at[h, k], sibling) for k in order0 for h in range(2)}

    mom_load = load(mom, mom_v)
    lr_load = load(lr, lr_v)
    rqr_load = load(rqr, rqr_v)
    rkvr_load = load(rkvr, rkvr_v)
    rest = [load(lf, lf_v), load(rq, rq_v), load(rkv, rkv_v)]

    def pair_sum(h, k, part_of):
        return own[h, k, part_of].astype(f32) + sib[h, k, part_of].astype(f32)

    low, high = slice(0, 2), slice(2, 4)
    ahead, behind = 1, SIDE - 1
    relay = {}
    for h in range(2):
        mine[h, 2].wait()
        pair[h, 2].wait_recv()
        part[h, 2] = pair_sum(h, 2, slice(0, 4)).astype(bf16)
        relay[h, 0] = send(part.at[h, 2, low], relayed.at[h, 0], first[h][ahead])
        relay[h, 1] = send(part.at[h, 2, high], relayed.at[h, 1], first[h][behind])
    near = []
    for h in range(2):
        for side, k, free in ((0, ahead, high), (1, behind, low)):
            mine[h, k].wait()
            pair[h, k].wait_recv()
            part[h, k, free] = pair_sum(h, k, free).astype(bf16)
            near.append(send(part.at[h, k, free], recv1.at[h, side, free], first[h][k]))
    for h in range(2):
        for side, k, held in ((0, ahead, low), (1, behind, high)):
            relay[h, side].wait_recv()
            value = pair_sum(h, k, held) + relayed[h, side].astype(f32)
            part[h, k, held] = value.astype(bf16)
            near.append(send(part.at[h, k, held], recv1.at[h, side, held], first[h][k]))
    for h in range(2):
        mine[h, 0].wait()
        pair[h, 0].wait_recv()
        acc[h] = pair_sum(h, 0, slice(0, 4))
    for copy in near:
        copy.wait_recv()

    def line_sum(h, k):
        j = (ys if h == 0 else xs)[k]
        return acc[h, j] + recv1[h, 0, j].astype(f32) + recv1[h, 1, j].astype(f32)

    step2 = {}
    for k in FAR_FIRST:
        for h in range(2):
            part2[h, k - 1] = line_sum(h, k).astype(bf16)
            step2[h, k] = send(part2.at[h, k - 1], recv2.at[h, k - 1], second[h][k])
    for h in range(2):
        value = line_sum(h, 0)
        for k in FAR_FIRST:
            step2[h, k].wait_recv()
        for i in range(SIDE - 1):
            value = value + recv2[h, i].astype(f32)
        total[x, y, core, h] = value.astype(bf16)

    def one(ref, h, p, r):
        return ref.at[xs[p], ys[r], core, 0] if h == 0 else ref.at[xs[r], ys[p], core, 1]

    def gather(ref, hooks):
        across = {}
        along = {}
        onward = {}
        forwards = []
        halves = range(2)

        def spread(h, r):
            block = one(ref, h, 0, r)
            for p in (ahead, behind):
                along[h, p, r] = send(block, block, first[h][p])

        def pass_on(h, p, r):
            block = one(ref, h, SIDE - p, r)
            onward[h, p, r] = send(block, block, first[h][p])

        def hand_over(h, p):
            block = group(ref, h, p, core)
            forwards.append(send(block, block, sibling))

        for k in FAR_FIRST:
            for h in halves:
                block = one(ref, h, 0, 0)
                across[h, k] = send(block, block, second[h][k])
        for h in halves:
            spread(h, 0)
        hooks[0]()
        for k in (ahead, behind):
            for h in halves:
                across[h, k].wait_recv()
                spread(h, SIDE - k)
        hooks[1]()
        for h in halves:
            along[h, ahead, 0].wait_recv()
            pass_on(h, ahead, 0)
        for h in halves:
            across[h, 2].wait_recv()
            spread(h, 2)
        hooks[2]()
        for h in halves:
            hand_over(h, 0)
        for r in (behind, ahead):
            for h in halves:
                along[h, behind, r].wait_recv()
                pass_on(h, behind, r)
        hooks[3]()
        for h in halves:
            along[h, ahead, 2].wait_recv()
            pass_on(h, ahead, 2)
        for h in halves:
            for r in (ahead, behind):
                along[h, ahead, r].wait_recv()
            hand_over(h, behind)
        for h in halves:
            for r in (0, 2):
                along[h, behind, r].wait_recv()
            hand_over(h, ahead)
        hooks[4]()
        for h in halves:
            for p, r in ((ahead, 0), (behind, behind), (behind, ahead), (ahead, 2)):
                onward[h, p, r].wait_recv()
            hand_over(h, 2)
        hooks[5]()
        for copy in forwards:
            copy.wait_recv()

    lane = lax.broadcasted_iota(jnp.int32, (1, 2 * KC), 1)
    is_key = lane < KC

    def to_lanes(square):
        column = jnp.sum(square, axis=0, keepdims=True)
        query = column[:, :128]
        for i in range(1, QC // 128):
            query = query + column[:, 128 * i : 128 * (i + 1)]
        return query, column[:, QC:]

    saved = {}

    def graft_part():
        mom_load.wait()
        row_grad = total[x, y, core].reshape(PANEL, COLS).astype(f32)
        moment_new = moment_keep * mom_v[...] + moment_add * row_grad * row_grad
        mom_new[...] = moment_new
        graft = row_grad / (jnp.sqrt(moment_new) + graft_eps)
        graft_q, graft_kv = to_lanes(jnp.square(graft))
        norm[0] = jnp.zeros((8, 128), f32)
        norm[0, 0:1, :] = graft_q
        norm[0, 1:2, :] = graft_kv

    def diagonal_part():
        rkvr_load.wait()
        row = lax.broadcasted_iota(jnp.int32, (KC, 2 * KC), 0)
        col = lax.broadcasted_iota(jnp.int32, (KC, 2 * KC), 1)
        for i in range(2):
            place = (col == row + i * KC).astype(f32).astype(bf16)
            diag[KC * i : KC * (i + 1), :] = dot(rkvr_v[i], place).astype(bf16)

    def nothing():
        pass

    def wait_loads():
        lr_load.wait()
        rqr_load.wait()
        for copy in rest:
            copy.wait()

    gather(total, (graft_part, diagonal_part, nothing, wait_loads, nothing, nothing))

    grad_q = total[..., :QC].reshape(ORDER, QC)
    grad_kv = total[..., QC:].reshape(ORDER, 2 * KC)
    proj_q = dot(lr_v[0], grad_q).astype(bf16)
    both = dot(lr_v[1:3].reshape(2 * PANEL, ORDER), grad_kv)
    proj_kv = jnp.where(is_key, both[:PANEL], both[PANEL:]).astype(bf16)
    cond_q = dot(proj_q, rqr_v[...])
    cond_kv = dot(proj_kv, diag[...])
    gathered[x, y, core, :, :, :QC] = cond_q.astype(bf16).reshape(2, HALF, QC)
    gathered[x, y, core, :, :, QC:] = cond_kv.astype(bf16).reshape(2, HALF, 2 * KC)

    def norm_start():
        square = jnp.square(jnp.concatenate([cond_q, cond_kv], axis=1))
        cond_lanes_q, cond_lanes_kv = to_lanes(square)
        norm[0, 2:3, :] = cond_lanes_q
        norm[0, 3:4, :] = cond_lanes_kv
        saved["y"] = [send(norm.at[0], norm_in.at[k - 1], on_y[k]) for k in FAR_FIRST]
        left_kv()

    def left_kv():
        owned_kv = total[x, y, core].reshape(PANEL, COLS)[:, QC:].astype(f32)
        split = jnp.concatenate(
            [jnp.where(is_key, owned_kv, 0.0), jnp.where(is_key, 0.0, owned_kv)], axis=0
        ).astype(bf16)
        both = dot(split, grad_kv, 1, 1)
        left_new[1] = factor_keep * lf_v[1] + factor_add * both[:PANEL]
        left_new[2] = factor_keep * lf_v[2] + factor_add * both[PANEL:]

    def norm_next():
        for copy in saved["y"]:
            copy.wait_recv()
        norm[1] = norm[0] + norm_in[0] + norm_in[1] + norm_in[2]
        saved["x"] = [send(norm.at[1], norm_in.at[2 + k], on_x[k]) for k in FAR_FIRST]

    def norm_pair():
        for copy in saved["x"]:
            copy.wait_recv()
        norm[2] = norm[1] + norm_in[3] + norm_in[4] + norm_in[5]
        saved["c"] = send(norm.at[2], norm_in.at[6], sibling)
        owned_q = total[x, y, core].reshape(PANEL, COLS)[:, :QC]
        left_new[0] = factor_keep * lf_v[0] + factor_add * dot(owned_q, grad_q, 1, 1)

    def norm_line():
        saved["c"].wait_recv()
        norm[3] = norm[2] + norm_in[6]
        saved["z"] = [send(norm.at[3], norm_z.at[k - 1], on_z[k]) for k in range(1, depth)]

    def right_q_part():
        columns = pl.ds(pl.multiple_of(x * 128, 128), 128)
        slab[...] = dot(total[..., columns].reshape(ORDER, 128), grad_q, 0, 0)
        mine_q = pl.ds(pl.multiple_of(lax.rem(dp, 2 * SIDE) * 16, 16), 16)
        rq_new[...] = factor_keep * rq_v[...] + factor_add * slab[mine_q, :]

    def right_kv_part():
        square = dot(grad_kv, grad_kv, 0, 0)
        rkv_new[0] = factor_keep * rkv_v[0] + factor_add * square[:KC, :KC]
        moved = pltpu.roll(square, KC, 1)
        rkv_new[1] = factor_keep * rkv_v[1] + factor_add * moved[KC:, :KC]

    gather(gathered, (norm_start, norm_next, norm_pair, norm_line, right_q_part, right_kv_part))

    for copy in saved["z"]:
        copy.wait_recv()
    sums = norm[3] + jnp.sum(norm_z[...], axis=0)

    def whole(row_index, mask):
        values = sums[row_index : row_index + 1, :]
        if mask is not None:
            values = jnp.where(mask, values, 0.0)
        return jnp.sum(values, axis=1, keepdims=True)

    def scale(graft_sq, shampoo_sq):
        return jnp.sqrt(graft_sq / (shampoo_sq + norm_eps))

    scale_q = scale(whole(0, None), whole(2, None))
    scale_k = scale(whole(1, is_key), whole(3, is_key))
    scale_v = scale(whole(1, lane >= KC), whole(3, lane >= KC))
    scale_row[:, :QC] = jnp.broadcast_to(scale_q, (8, QC))
    scale_row[:, QC:] = jnp.broadcast_to(jnp.where(is_key, scale_k, scale_v), (8, 2 * KC))

    assert len(started) == ssem.shape[0]
    for copy in started:
        copy.wait_send()


def finish(gathered, scale_row, left, rq, rkv, mom, direction, left_out, rq_out, rkv_out, mom_out, rows, sem):
    copies = []

    def store(src, dst):
        copy = pltpu.make_async_copy(src, dst, sem.at[len(copies)])
        copy.start()
        copies.append(copy)

    for src, dst in ((left, left_out), (mom, mom_out), (rq, rq_out), (rkv, rkv_out)):
        store(src, dst)
    height = ORDER // SIDE
    scale = scale_row[0:1, :]
    for i in range(SIDE):
        rows[i] = (gathered[i].reshape(height, COLS).astype(f32) * scale).astype(bf16)
        store(rows.at[i], direction.at[pl.ds(i * height, height)])
    for copy in copies:
        copy.wait()


def local_step(grads, left_factor, left_root, right_q, right_kv, right_q_root, right_kv_root, moment):
    depth = lax.axis_size("mp")
    grid = (SIDE, SIDE, 2, 2, HALF, COLS)
    block = (SIDE, HALF, COLS)
    n_sends = 8 + 18 + 2 * 38 + 7 + depth - 1
    hbm = pl.BlockSpec(memory_space=pltpu.HBM)
    vmem = pl.BlockSpec(memory_space=pltpu.VMEM)
    shape = jax.ShapeDtypeStruct
    gathered, scale_row, left_new, rq_new, rkv_new, mom_new = pl.pallas_call(
        lambda *refs: kernel(depth, *refs),
        out_shape=(
            shape(grid, bf16),
            shape((8, COLS), f32),
            shape((3, PANEL, ORDER), f32),
            shape((16, QC), f32),
            shape((2, KC, KC), f32),
            shape((PANEL, COLS), f32),
        ),
        in_specs=[hbm] * 8,
        out_specs=(vmem,) * 6,
        scratch_shapes=[
            pltpu.VMEM((2, SIDE) + block, bf16),
            pltpu.VMEM((2, SIDE) + block, bf16),
            pltpu.VMEM((2, SIDE) + block, bf16),
            pltpu.VMEM((2, 2, 2, HALF, COLS), bf16),
            pltpu.VMEM((2, 2) + block, bf16),
            pltpu.VMEM((2,) + block, f32),
            pltpu.VMEM((2, SIDE - 1, HALF, COLS), bf16),
            pltpu.VMEM((2, SIDE - 1, HALF, COLS), bf16),
            pltpu.VMEM(grid, bf16),
            pltpu.VMEM((3, PANEL, ORDER), f32),
            pltpu.VMEM((3, PANEL, ORDER), bf16),
            pltpu.VMEM((16, QC), f32),
            pltpu.VMEM((2, KC, KC), f32),
            pltpu.VMEM((QC, QC), bf16),
            pltpu.VMEM((2, KC, KC), bf16),
            pltpu.VMEM((PANEL, COLS), f32),
            pltpu.VMEM((2 * KC, 2 * KC), bf16),
            pltpu.VMEM((128, QC), f32),
            pltpu.VMEM((4, 8, 128), f32),
            pltpu.VMEM((7, 8, 128), f32),
            pltpu.VMEM((depth - 1, 8, 128), f32),
            pltpu.SemaphoreType.DMA((n_sends,)),
            pltpu.SemaphoreType.DMA((n_sends,)),
            pltpu.SemaphoreType.DMA((15,)),
        ],
        compiler_params=pltpu.CompilerParams(
            collective_id=0, has_side_effects=True, vmem_limit_bytes=40 * 1024 * 1024
        ),
    )(
        *(
            pltpu.with_memory_space_constraint(array, pltpu.HBM)
            for array in (
                grads.reshape(grid), left_factor[0], left_root[0], right_q[0], right_kv[0],
                right_q_root[0], right_kv_root[0], moment,
            )
        )
    )
    direction, left_new, rq_new, rkv_new, mom_new = pl.pallas_call(
        finish,
        out_shape=(
            shape((ORDER, COLS), bf16),
            shape((3, PANEL, ORDER), f32),
            shape((16, QC), f32),
            shape((2, KC, KC), f32),
            shape((PANEL, COLS), f32),
        ),
        in_specs=[vmem] * 6,
        out_specs=(hbm,) * 5,
        scratch_shapes=[
            pltpu.VMEM((SIDE, ORDER // SIDE, COLS), bf16),
            pltpu.SemaphoreType.DMA((4 + SIDE,)),
        ],
        compiler_params=pltpu.CompilerParams(vmem_limit_bytes=40 * 1024 * 1024),
    )(gathered, scale_row, left_new, rq_new, rkv_new, mom_new)
    return direction, left_new[None], rq_new[None], rkv_new[None], mom_new


def solution(mesh):
    return jax.shard_map(
        local_step,
        mesh=mesh,
        in_specs=(
            P("dp", None, "mp"),
            P("mp", None, "dp", None),
            P("mp", None, "dp", None),
            P("mp", "dp", None),
            P("mp", None, None, None),
            P("mp", None, None),
            P("mp", None, None, None),
            P("dp", "mp"),
        ),
        out_specs=(
            P(None, "mp"),
            P("mp", None, "dp", None),
            P("mp", "dp", None),
            P("mp", None, None, None),
            P("dp", "mp"),
        ),
        check_vma=False,
    )
```

time: 337 us -> 60.1 us (0.18)
  waiting for transfers between devices: 194 us -> 0 us
  blocking collectives: 105 us -> 0 us
  Pallas kernels: 0 us -> 59.3 us
  between operations: 14.2 us -> 0.64 us
  other arithmetic: 10.9 us -> 0 us
  matrix products: 8.68 us -> 0 us
    psum x1 -> x0, waiting for transfers between devices: 144 us -> none  [local(): summed = lax.psum(grads[0].astype(jnp.float32).astype(jnp.bfloat16), 'dp')]
    psum x1 -> x0, blocking collectives: 105 us -> none  [local(): graft_sq, shampoo_sq = lax.psum((graft_terms, shampoo_terms), ('dp', 'mp'))]
    pallas_call x0 -> x2, Pallas kernels: none -> 59.3 us  [the longest x1 58 us: local_step(): pl.pallas_call(lambda *refs: kernel(depth, *refs), out_shape=(shape(grid,...]
    all_gather x1 -> x0, waiting for transfers between devices: 49.1 us -> none  [local(): direction = lax.all_gather(rows_out, 'dp', axis=0, tiled=True)]
    dot_general x9 -> x0, matrix products: 8.68 us -> none  [the longest x3 6.15 us: local(): jnp.dot(projected, root_block, preferred_element_type=jnp.float32)]
    another operation x4 -> x0, other arithmetic: 6.02 us -> none  [the longest x1 4.07 us: local(): jnp.stack([jnp.sum(jnp.square(graft[:, offset:offset + extent])) for offs...]
  transfers between devices with their start and end apart: 2 -> 0, of which waited for: 2 -> 0; matrix products, arithmetic and copies ran while one was open for 1% -> 0% of each run, Pallas kernels for 0% -> 0%
where the time goes in v1:
time: 60.1 us; the launch traced here: 60 us
  Pallas kernels  59.3 us (99%)
  between operations  0.64 us (1%)
    pallas_call x1, Pallas kernels, local_step(): pl.pallas_call(lambda *refs: kernel(depth, *refs), out_shape=(shape(grid,...  58 us
    pallas_call x1, Pallas kernels, local_step(): pl.pallas_call(finish, out_shape=(shape((ORDER, COLS), bf16), shape((3, P...  1.31 us

profile of v1, /device:TPU:1, one launch (start us, length us, event | category | flops | bytes accessed | tf_op | source)
XLA Modules:
  0.0 60.0 jit_solution(18282403537396872406)
XLA Ops:
  0.6 58.0 %shard_map.119 = (bf16[4,4,2,2,16,640]{5,4,3,2,1,0:T(8,128)(2,1)S(1)}, f32[8,640]{1,0:T(8,128)S(1)}, f32[3,32,1024]{2,1,0:T(8,128)S(1)}, f32[16,512]{1,0:T(8,128...) custom-call(bf16[4,4,2,2,16,640]{5,4,3,2,1,0:T(8,128)(2,1)} %bitcast.10, f32[3,32,1024]{2,1,0:T(8,128)} %bitcast.12, ...), custom_call_target="tpu_custom_call" | custom-call | tf_op jit(solution)/shard_map/pallas_call | solution.py:371
  58.7 1.3 %shard_map.120 = (bf16[1024,640]{1,0:T(8,128)(2,1)}, f32[3,32,1024]{2,1,0:T(8,128)}, f32[16,512]{1,0:T(8,128)}, f32[2,64,64]{2,1,0:T(8,128)}, f32[32,640]{1,0:T(8,128)}) custom-call(bf16[4,4,2,2,16,640]{5,4,3,2,1,0:T(8,128)(2,1)S(1)} %get-tuple-element.16.gathered, f32[8,640]{1,0:T(8,128)S(1)} %get-tuple-element.17.scale_row, ...), custom_call_target="tpu_custom_call" | custom-call | tf_op jit(solution)/shard_map/pallas_call | solution.py:421

commit v2 on v1

v2 whole, which is shorter than its diff:
```python
import jax
import jax.numpy as jnp
from jax import lax
from jax.experimental import pallas as pl
from jax.experimental.pallas import tpu as pltpu
from jax.sharding import PartitionSpec as P

MESH = pl.DeviceIdType.MESH
f32 = jnp.float32
bf16 = jnp.bfloat16

factor_keep = 0.95
factor_add = 0.05
moment_keep = 0.99
moment_add = 0.01
graft_eps = 1e-08
norm_eps = 1e-06

SIDE = 4
HALF = 16
QC = 512
KC = 64
COLS = QC + 2 * KC
ORDER = 1024
PANEL = 32
FAR_FIRST = (2, 1, 3)


def dot(a, b, ca=1, cb=0):
    return lax.dot_general(a, b, (((ca,), (cb,)), ((), ())), preferred_element_type=f32)


def kernel(
    g, lf, lr, rq, rkv, rqr, rkvr, mom,
    gathered, scale_row, left_new, rq_new, rkv_new, mom_new,
    own, sib, part, recv1, acc, part2, recv2, total,
    lf_v, lr_v, rq_v, rkv_v, rqr_v, rkvr_v, mom_v,
    diag, slab, norm, norm_in,
    ssem, rsem, lsem,
):
    dp = lax.axis_index("dp")
    z = lax.axis_index("mp")
    core = lax.rem(dp, 2)
    other = 1 - core
    y = lax.rem(dp // 2, SIDE)
    x = dp // (2 * SIDE)
    z_low = lax.rem(z, SIDE)
    z_high = z // SIDE

    def at(i, j, k):
        return ((i * SIDE + j) * 2 + k, z)

    def ring(v):
        return [v] + [lax.rem(v + k, SIDE) for k in range(1, SIDE)]

    sibling = at(x, y, other)
    xs, ys = ring(x), ring(y)
    others = range(1, SIDE)
    on_x = [None] + [at(xs[k], y, core) for k in others]
    on_y = [None] + [at(x, ys[k], core) for k in others]
    first = (on_x, on_y)
    second = (on_y, on_x)
    crossed = [at(x, ys[k], other) for k in others]
    on_low = [(dp, z_high * SIDE + v) for v in ring(z_low)[1:]]
    on_high = [(dp, v * SIDE + z_low) for v in ring(z_high)[1:]]

    barrier = pltpu.get_barrier_semaphore()
    partners = [sibling] + on_x[1:] + on_y[1:] + crossed + on_low + on_high
    for device in partners:
        pl.semaphore_signal(barrier, inc=1, device_id=device, device_id_type=MESH)

    local = []

    def load(src, dst):
        copy = pltpu.make_async_copy(src, dst, lsem.at[len(local)])
        copy.start()
        local.append(copy)
        return copy

    mine = [load(g.at[:, :, core, h], own.at[h]) for h in range(2)]
    pl.semaphore_wait(barrier, len(partners))

    sends = {}
    arrivals = {}

    def send(src, dst, device, outgoing, incoming):
        i = sends.setdefault(outgoing, len(sends))
        j = arrivals.setdefault(incoming, len(arrivals))
        pltpu.make_async_remote_copy(
            src_ref=src, dst_ref=dst, send_sem=ssem.at[i], recv_sem=rsem.at[j],
            device_id=device, device_id_type=MESH,
        ).start()

    def all_of(ref, outgoing=None, incoming=None):
        copy = pltpu.make_async_remote_copy(
            src_ref=ref, dst_ref=ref,
            send_sem=ssem.at[sends[outgoing] if outgoing else 0],
            recv_sem=rsem.at[arrivals[incoming] if incoming else 0],
            device_id=sibling, device_id_type=MESH,
        )
        if outgoing:
            copy.wait_send()
        else:
            copy.wait_recv()

    def group(ref, h, k, c):
        return ref.at[xs[k], :, c, 0] if h == 0 else ref.at[:, ys[k], c, 1]

    for h in range(2):
        send(g.at[:, :, other, h], sib.at[h], sibling, "pair", ("pair", h))

    mom_load = load(mom, mom_v)
    lr_load = load(lr, lr_v)
    rqr_load = load(rqr, rqr_v)
    rkvr_load = load(rkvr, rkvr_v)
    rest = [load(lf, lf_v), load(rq, rq_v), load(rkv, rkv_v)]

    for h in range(2):
        mine[h].wait()
        all_of(sib.at[h], incoming=("pair", h))

        def pair_sum(k):
            if h == 0:
                return own[h, xs[k]].astype(f32) + sib[h, xs[k]].astype(f32)
            return own[h, :, ys[k]].astype(f32) + sib[h, :, ys[k]].astype(f32)

        for k in FAR_FIRST:
            part[h, k - 1] = pair_sum(k).astype(bf16)
            send(part.at[h, k - 1], recv1.at[h, k - 1], first[h][k], "step1", ("step1", h))
        acc[h] = pair_sum(0)

    kept = []
    for h in range(2):
        all_of(recv1.at[h], incoming=("step1", h))

        def line_sum(k):
            j = (ys if h == 0 else xs)[k]
            value = acc[h, j]
            for i in range(SIDE - 1):
                value = value + recv1[h, i, j].astype(f32)
            return value

        for k in FAR_FIRST:
            part2[h, k - 1] = line_sum(k).astype(bf16)
            send(part2.at[h, k - 1], recv2.at[h, k - 1], second[h][k], "step2", ("step2", h))
        kept.append(line_sum(0))
    three = recv2.at[0]
    for h in range(2):
        value = kept[h]
        all_of(recv2.at[h], incoming=("step2", h))
        for i in range(SIDE - 1):
            value = value + recv2[h, i].astype(f32)
        total[x, y, core, h] = value.astype(bf16)
        for k in FAR_FIRST:
            block = total.at[x, y, core, h]
            send(block, block, second[h][k], "across0", ("across0", h))

    def gather(ref, name, early, middle, late):
        early()
        for h in range(2):
            all_of(three, incoming=("across" + name, h))
            block = group(ref, h, 0, core)
            for k in FAR_FIRST:
                send(block, block, first[h][k], "along" + name, ("along" + name, h, k))
        for h in range(2):
            block = group(ref, h, 0, core)
            send(block, block, sibling, "over" + name, "over" + name)
        middle()
        for k in (1, 3, 2):
            for h in range(2):
                block = group(ref, h, SIDE - k, core)
                all_of(block, incoming=("along" + name, h, k))
                send(block, block, sibling, "over" + name, "over" + name)
        late()
        all_of(ref.at[:, :, other], incoming="over" + name)

    lane = lax.broadcasted_iota(jnp.int32, (1, 2 * KC), 1)
    is_key = lane < KC

    def to_lanes(square):
        column = jnp.sum(square, axis=0, keepdims=True)
        query = column[:, :128]
        for i in range(1, QC // 128):
            query = query + column[:, 128 * i : 128 * (i + 1)]
        return query, column[:, QC:]

    def graft_part():
        mom_load.wait()
        row_grad = total[x, y, core].reshape(PANEL, COLS).astype(f32)
        moment_new = moment_keep * mom_v[...] + moment_add * row_grad * row_grad
        mom_new[...] = moment_new
        graft = row_grad / (jnp.sqrt(moment_new) + graft_eps)
        graft_q, graft_kv = to_lanes(jnp.square(graft))
        norm[0] = jnp.zeros((8, 128), f32)
        norm[0, 0:1, :] = graft_q
        norm[0, 1:2, :] = graft_kv

    def diagonal_part():
        rkvr_load.wait()
        row = lax.broadcasted_iota(jnp.int32, (KC, 2 * KC), 0)
        col = lax.broadcasted_iota(jnp.int32, (KC, 2 * KC), 1)
        for i in range(2):
            place = (col == row + i * KC).astype(f32).astype(bf16)
            diag[KC * i : KC * (i + 1), :] = dot(rkvr_v[i], place).astype(bf16)

    def wait_loads():
        lr_load.wait()
        rqr_load.wait()
        for copy in rest:
            copy.wait()

    gather(total, "0", graft_part, diagonal_part, wait_loads)

    def query_grad():
        return total[..., :QC].reshape(ORDER, QC)

    def key_value_grad():
        return total[..., QC:].reshape(ORDER, 2 * KC)

    proj_q = dot(lr_v[0], query_grad()).astype(bf16)
    both = dot(lr_v[1:3].reshape(2 * PANEL, ORDER), key_value_grad())
    proj_kv = jnp.where(is_key, both[:PANEL], both[PANEL:]).astype(bf16)
    cond_q = dot(proj_q, rqr_v[...])
    cond_kv = dot(proj_kv, diag[...])
    gathered[x, y, core, :, :, :QC] = cond_q.astype(bf16).reshape(2, HALF, QC)
    gathered[x, y, core, :, :, QC:] = cond_kv.astype(bf16).reshape(2, HALF, 2 * KC)
    for h in range(2):
        for k in FAR_FIRST:
            block = gathered.at[x, y, core, h]
            send(block, block, second[h][k], "across1", ("across1", h))

    levels = (
        (0, 2 * SIDE, 2 * y + core, on_y[1:] + [sibling] + crossed),
        (2 * SIDE, SIDE, x, on_x[1:]),
        (3 * SIDE, SIDE, z_low, on_low),
        (4 * SIDE, SIDE, z_high, on_high),
    )

    def norm_send(level):
        start, _, place, devices = levels[level]
        norm_in[start + place] = norm[level]
        for device in devices:
            send(norm.at[level], norm_in.at[start + place], device, "norm", ("norm", level))

    def norm_add(level):
        start, count, _, _ = levels[level]
        all_of(norm_in.at[start : start + count - 1], incoming=("norm", level))
        value = norm_in[start]
        for i in range(1, count):
            value = value + norm_in[start + i]
        return value

    def norm_step(level):
        norm[level] = norm_add(level - 1)
        norm_send(level)

    def norm_start():
        square = jnp.square(jnp.concatenate([cond_q, cond_kv], axis=1))
        cond_lanes_q, cond_lanes_kv = to_lanes(square)
        norm[0, 2:3, :] = cond_lanes_q
        norm[0, 3:4, :] = cond_lanes_kv
        norm_send(0)

    def left_part():
        owned = total[x, y, core].reshape(PANEL, COLS)
        owned_kv = owned[:, QC:].astype(f32)
        split = jnp.concatenate(
            [jnp.where(is_key, owned_kv, 0.0), jnp.where(is_key, 0.0, owned_kv)], axis=0
        ).astype(bf16)
        both = dot(split, key_value_grad(), 1, 1)
        left_new[1] = factor_keep * lf_v[1] + factor_add * both[:PANEL]
        left_new[2] = factor_keep * lf_v[2] + factor_add * both[PANEL:]
        left_new[0] = factor_keep * lf_v[0] + factor_add * dot(owned[:, :QC], query_grad(), 1, 1)

    def right_part():
        columns = pl.ds(pl.multiple_of(x * 128, 128), 128)
        slab[...] = dot(total[..., columns].reshape(ORDER, 128), query_grad(), 0, 0)
        mine_q = pl.ds(pl.multiple_of(lax.rem(dp, 2 * SIDE) * 16, 16), 16)
        rq_new[...] = factor_keep * rq_v[...] + factor_add * slab[mine_q, :]
        square = dot(key_value_grad(), key_value_grad(), 0, 0)
        rkv_new[0] = factor_keep * rkv_v[0] + factor_add * square[:KC, :KC]
        moved = pltpu.roll(square, KC, 1)
        rkv_new[1] = factor_keep * rkv_v[1] + factor_add * moved[KC:, :KC]

    def middle_part():
        norm_step(1)
        left_part()
        norm_step(2)
        right_part()
        norm_step(3)

    def scale_part():
        sums = norm_add(3)

        def whole(row_index, mask):
            values = sums[row_index : row_index + 1, :]
            if mask is not None:
                values = jnp.where(mask, values, 0.0)
            return jnp.sum(values, axis=1, keepdims=True)

        def scale(graft_sq, shampoo_sq):
            return jnp.sqrt(graft_sq / (shampoo_sq + norm_eps))

        scale_q = scale(whole(0, None), whole(2, None))
        scale_k = scale(whole(1, is_key), whole(3, is_key))
        scale_v = scale(whole(1, lane >= KC), whole(3, lane >= KC))
        scale_row[:, :QC] = jnp.broadcast_to(scale_q, (8, QC))
        scale_row[:, QC:] = jnp.broadcast_to(jnp.where(is_key, scale_k, scale_v), (8, 2 * KC))

    gather(gathered, "1", norm_start, middle_part, scale_part)

    all_of(sib, outgoing="pair")
    all_of(recv1, outgoing="step1")
    all_of(recv2, outgoing="step2")
    for name, ref in (("0", total), ("1", gathered)):
        all_of(recv2, outgoing="across" + name)
        all_of(recv1, outgoing="along" + name)
        all_of(ref.at[:, :, core], outgoing="over" + name)
    all_of(norm_in.at[: 4 * SIDE], outgoing="norm")
    assert len(sends) == ssem.shape[0] and len(arrivals) == rsem.shape[0]


def finish(gathered, scale_row, left, rq, rkv, mom, direction, left_out, rq_out, rkv_out, mom_out, rows, sem):
    copies = []

    def store(src, dst):
        copy = pltpu.make_async_copy(src, dst, sem.at[len(copies)])
        copy.start()
        copies.append(copy)

    for src, dst in ((left, left_out), (mom, mom_out), (rq, rq_out), (rkv, rkv_out)):
        store(src, dst)
    height = ORDER // SIDE
    scale = scale_row[0:1, :]
    for i in range(SIDE):
        rows[i] = (gathered[i].reshape(height, COLS).astype(f32) * scale).astype(bf16)
        store(rows.at[i], direction.at[pl.ds(i * height, height)])
    for copy in copies:
        copy.wait()


def local_step(grads, left_factor, left_root, right_q, right_kv, right_q_root, right_kv_root, moment):
    grid = (SIDE, SIDE, 2, 2, HALF, COLS)
    block = (SIDE, HALF, COLS)
    hbm = pl.BlockSpec(memory_space=pltpu.HBM)
    vmem = pl.BlockSpec(memory_space=pltpu.VMEM)
    shape = jax.ShapeDtypeStruct
    gathered, scale_row, left_new, rq_new, rkv_new, mom_new = pl.pallas_call(
        kernel,
        out_shape=(
            shape(grid, bf16),
            shape((8, COLS), f32),
            shape((3, PANEL, ORDER), f32),
            shape((16, QC), f32),
            shape((2, KC, KC), f32),
            shape((PANEL, COLS), f32),
        ),
        in_specs=[hbm] * 8,
        out_specs=(vmem,) * 6,
        scratch_shapes=[
            pltpu.VMEM((2, SIDE) + block, bf16),
            pltpu.VMEM((2, SIDE) + block, bf16),
            pltpu.VMEM((2, SIDE - 1) + block, bf16),
            pltpu.VMEM((2, SIDE - 1) + block, bf16),
            pltpu.VMEM((2,) + block, f32),
            pltpu.VMEM((2, SIDE - 1, HALF, COLS), bf16),
            pltpu.VMEM((2, SIDE - 1, HALF, COLS), bf16),
            pltpu.VMEM(grid, bf16),
            pltpu.VMEM((3, PANEL, ORDER), f32),
            pltpu.VMEM((3, PANEL, ORDER), bf16),
            pltpu.VMEM((16, QC), f32),
            pltpu.VMEM((2, KC, KC), f32),
            pltpu.VMEM((QC, QC), bf16),
            pltpu.VMEM((2, KC, KC), bf16),
            pltpu.VMEM((PANEL, COLS), f32),
            pltpu.VMEM((2 * KC, 2 * KC), bf16),
            pltpu.VMEM((128, QC), f32),
            pltpu.VMEM((4, 8, 128), f32),
            pltpu.VMEM((5 * SIDE, 8, 128), f32),
            pltpu.SemaphoreType.DMA((10,)),
            pltpu.SemaphoreType.DMA((28,)),
            pltpu.SemaphoreType.DMA((9,)),
        ],
        compiler_params=pltpu.CompilerParams(
            collective_id=0, has_side_effects=True, vmem_limit_bytes=40 * 1024 * 1024
        ),
    )(
        *(
            pltpu.with_memory_space_constraint(array, pltpu.HBM)
            for array in (
                grads.reshape(grid), left_factor[0], left_root[0], right_q[0], right_kv[0],
                right_q_root[0], right_kv_root[0], moment,
            )
        )
    )
    direction, left_new, rq_new, rkv_new, mom_new = pl.pallas_call(
        finish,
        out_shape=(
            shape((ORDER, COLS), bf16),
            shape((3, PANEL, ORDER), f32),
            shape((16, QC), f32),
            shape((2, KC, KC), f32),
            shape((PANEL, COLS), f32),
        ),
        in_specs=[vmem] * 6,
        out_specs=(hbm,) * 5,
        scratch_shapes=[
            pltpu.VMEM((SIDE, ORDER // SIDE, COLS), bf16),
            pltpu.SemaphoreType.DMA((4 + SIDE,)),
        ],
        compiler_params=pltpu.CompilerParams(vmem_limit_bytes=40 * 1024 * 1024),
    )(gathered, scale_row, left_new, rq_new, rkv_new, mom_new)
    return direction, left_new[None], rq_new[None], rkv_new[None], mom_new


def solution(mesh):
    return jax.shard_map(
        local_step,
        mesh=mesh,
        in_specs=(
            P("dp", None, "mp"),
            P("mp", None, "dp", None),
            P("mp", None, "dp", None),
            P("mp", "dp", None),
            P("mp", None, None, None),
            P("mp", None, None),
            P("mp", None, None, None),
            P("dp", "mp"),
        ),
        out_specs=(
            P(None, "mp"),
            P("mp", None, "dp", None),
            P("mp", "dp", None),
            P("mp", None, None, None),
            P("dp", "mp"),
        ),
        check_vma=False,
    )
```

time: 60.1 us -> 57.7 us (0.960)
  Pallas kernels: 59.3 us -> 56.8 us
    pallas_call x1, Pallas kernels: 58 us -> 55.5 us  [local_step(): pl.pallas_call(kernel, out_shape=(shape(grid, bf16), shape((8, COLS), f32...]
where the time goes in v2:
time: 57.7 us; the launch traced here: 57.4 us
  Pallas kernels  56.8 us (98%)
  between operations  0.64 us (1%)
    pallas_call x1, Pallas kernels, local_step(): pl.pallas_call(kernel, out_shape=(shape(grid, bf16), shape((8, COLS), f32...  55.5 us
    pallas_call x1, Pallas kernels, local_step(): pl.pallas_call(finish, out_shape=(shape((ORDER, COLS), bf16), shape((3, P...  1.31 us

profile of v2, /device:TPU:1, one launch (start us, length us, event | category | flops | bytes accessed | tf_op | source)
XLA Modules:
  0.0 57.4 jit_solution(3635002118469413185)
XLA Ops:
  0.6 55.5 %shard_map.119 = (bf16[4,4,2,2,16,640]{5,4,3,2,1,0:T(8,128)(2,1)S(1)}, f32[8,640]{1,0:T(8,128)S(1)}, f32[3,32,1024]{2,1,0:T(8,128)S(1)}, f32[16,512]{1,0:T(8,128...) custom-call(bf16[4,4,2,2,16,640]{5,4,3,2,1,0:T(8,128)(2,1)} %bitcast.10, f32[3,32,1024]{2,1,0:T(8,128)} %bitcast.12, ...), custom_call_target="tpu_custom_call" | custom-call | tf_op jit(solution)/shard_map/pallas_call | solution.py:348
  56.1 1.3 %shard_map.120 = (bf16[1024,640]{1,0:T(8,128)(2,1)}, f32[3,32,1024]{2,1,0:T(8,128)}, f32[16,512]{1,0:T(8,128)}, f32[2,64,64]{2,1,0:T(8,128)}, f32[32,640]{1,0:T(8,128)}) custom-call(bf16[4,4,2,2,16,640]{5,4,3,2,1,0:T(8,128)(2,1)S(1)} %get-tuple-element.16.gathered, f32[8,640]{1,0:T(8,128)S(1)} %get-tuple-element.17.scale_row, ...), custom_call_target="tpu_custom_call" | custom-call | tf_op jit(solution)/shard_map/pallas_call | solution.py:396

commit v3 on v2

--- a/solution.py
+++ b/solution.py
@@ -31,11 +31,11 @@
 
 
 def kernel(
-    g, lf, lr, rq, rkv, rqr, rkvr, mom,
-    gathered, scale_row, left_new, rq_new, rkv_new, mom_new,
-    own, sib, part, recv1, acc, part2, recv2, total,
-    lf_v, lr_v, rq_v, rkv_v, rqr_v, rkvr_v, mom_v,
-    diag, slab, norm, norm_in,
+    g, lr, rqr, rkvr, mom,
+    gathered, total, scale_row, mom_new,
+    own, sib, part, recv1, acc, part2, recv2,
+    lr_v, rqr_v, rkvr_v, mom_v,
+    diag, norm, norm_in,
     ssem, rsem, lsem,
 ):
     dp = lax.axis_index("dp")
@@ -113,7 +113,6 @@
     lr_load = load(lr, lr_v)
     rqr_load = load(rqr, rqr_v)
     rkvr_load = load(rkvr, rkvr_v)
-    rest = [load(lf, lf_v), load(rq, rq_v), load(rkv, rkv_v)]
 
     for h in range(2):
         mine[h].wait()
@@ -206,8 +205,6 @@
     def wait_loads():
         lr_load.wait()
         rqr_load.wait()
-        for copy in rest:
-            copy.wait()
 
     gather(total, "0", graft_part, diagonal_part, wait_loads)
 
@@ -261,32 +258,9 @@
         norm[0, 3:4, :] = cond_lanes_kv
         norm_send(0)
 
-    def left_part():
-        owned = total[x, y, core].reshape(PANEL, COLS)
-        owned_kv = owned[:, QC:].astype(f32)
-        split = jnp.concatenate(
-            [jnp.where(is_key, owned_kv, 0.0), jnp.where(is_key, 0.0, owned_kv)], axis=0
-        ).astype(bf16)
-        both = dot(split, key_value_grad(), 1, 1)
-        left_new[1] = factor_keep * lf_v[1] + factor_add * both[:PANEL]
-        left_new[2] = factor_keep * lf_v[2] + factor_add * both[PANEL:]
-        left_new[0] = factor_keep * lf_v[0] + factor_add * dot(owned[:, :QC], query_grad(), 1, 1)
-
-    def right_part():
-        columns = pl.ds(pl.multiple_of(x * 128, 128), 128)
-        slab[...] = dot(total[..., columns].reshape(ORDER, 128), query_grad(), 0, 0)
-        mine_q = pl.ds(pl.multiple_of(lax.rem(dp, 2 * SIDE) * 16, 16), 16)
-        rq_new[...] = factor_keep * rq_v[...] + factor_add * slab[mine_q, :]
-        square = dot(key_value_grad(), key_value_grad(), 0, 0)
-        rkv_new[0] = factor_keep * rkv_v[0] + factor_add * square[:KC, :KC]
-        moved = pltpu.roll(square, KC, 1)
-        rkv_new[1] = factor_keep * rkv_v[1] + factor_add * moved[KC:, :KC]
-
     def middle_part():
         norm_step(1)
-        left_part()
         norm_step(2)
-        right_part()
         norm_step(3)
 
     def scale_part():
@@ -320,23 +294,62 @@
     assert len(sends) == ssem.shape[0] and len(arrivals) == rsem.shape[0]
 
 
-def finish(gathered, scale_row, left, rq, rkv, mom, direction, left_out, rq_out, rkv_out, mom_out, rows, sem):
-    copies = []
-
-    def store(src, dst):
-        copy = pltpu.make_async_copy(src, dst, sem.at[len(copies)])
-        copy.start()
-        copies.append(copy)
-
-    for src, dst in ((left, left_out), (mom, mom_out), (rq, rq_out), (rkv, rkv_out)):
-        store(src, dst)
+def finish(
+    gathered, total, scale_row, mom, lf, rq, rkv,
+    direction, left_out, rq_out, rkv_out, mom_out,
+    rows, lf_v, rq_v, rkv_v, slab, sem,
+):
+    dp = lax.axis_index("dp")
+    x = dp // (2 * SIDE)
+    place = lax.rem(dp, 2 * SIDE)
+    count = [0]
+
+    def copy(src, dst):
+        made = pltpu.make_async_copy(src, dst, sem.at[count[0]])
+        count[0] += 1
+        made.start()
+        return made
+
+    loads = [copy(lf, lf_v), copy(rq, rq_v), copy(rkv, rkv_v)]
+    stores = [copy(mom, mom_out)]
     height = ORDER // SIDE
     scale = scale_row[0:1, :]
     for i in range(SIDE):
         rows[i] = (gathered[i].reshape(height, COLS).astype(f32) * scale).astype(bf16)
-        store(rows.at[i], direction.at[pl.ds(i * height, height)])
-    for copy in copies:
-        copy.wait()
+        stores.append(copy(rows.at[i], direction.at[pl.ds(i * height, height)]))
+
+    def query_grad():
+        return total[..., :QC].reshape(ORDER, QC)
+
+    def key_value_grad():
+        return total[..., QC:].reshape(ORDER, 2 * KC)
+
+    for made in loads:
+        made.wait()
+    is_key = lax.broadcasted_iota(jnp.int32, (1, 2 * KC), 1) < KC
+    owned = total[x, place // 2, lax.rem(place, 2)].reshape(PANEL, COLS)
+    owned_kv = owned[:, QC:].astype(f32)
+    split = jnp.concatenate(
+        [jnp.where(is_key, owned_kv, 0.0), jnp.where(is_key, 0.0, owned_kv)], axis=0
+    ).astype(bf16)
+    lf_v[0] = factor_keep * lf_v[0] + factor_add * dot(owned[:, :QC], query_grad(), 1, 1)
+    both = dot(split, key_value_grad(), 1, 1)
+    lf_v[1] = factor_keep * lf_v[1] + factor_add * both[:PANEL]
+    lf_v[2] = factor_keep * lf_v[2] + factor_add * both[PANEL:]
+    stores.append(copy(lf_v, left_out))
+
+    columns = pl.ds(pl.multiple_of(x * 128, 128), 128)
+    slab[...] = dot(total[..., columns].reshape(ORDER, 128), query_grad(), 0, 0)
+    mine_q = pl.ds(pl.multiple_of(place * 16, 16), 16)
+    rq_v[...] = factor_keep * rq_v[...] + factor_add * slab[mine_q, :]
+    stores.append(copy(rq_v, rq_out))
+    square = dot(key_value_grad(), key_value_grad(), 0, 0)
+    rkv_v[0] = factor_keep * rkv_v[0] + factor_add * square[:KC, :KC]
+    moved = pltpu.roll(square, KC, 1)
+    rkv_v[1] = factor_keep * rkv_v[1] + factor_add * moved[KC:, :KC]
+    stores.append(copy(rkv_v, rkv_out))
+    for made in stores:
+        made.wait()
 
 
 def local_step(grads, left_factor, left_root, right_q, right_kv, right_q_root, right_kv_root, moment):
@@ -345,18 +358,20 @@
     hbm = pl.BlockSpec(memory_space=pltpu.HBM)
     vmem = pl.BlockSpec(memory_space=pltpu.VMEM)
     shape = jax.ShapeDtypeStruct
-    gathered, scale_row, left_new, rq_new, rkv_new, mom_new = pl.pallas_call(
+
+    def stay(*arrays):
+        return tuple(pltpu.with_memory_space_constraint(array, pltpu.HBM) for array in arrays)
+
+    gathered, total, scale_row, mom_new = pl.pallas_call(
         kernel,
         out_shape=(
             shape(grid, bf16),
+            shape(grid, bf16),
             shape((8, COLS), f32),
-            shape((3, PANEL, ORDER), f32),
-            shape((16, QC), f32),
-            shape((2, KC, KC), f32),
             shape((PANEL, COLS), f32),
         ),
-        in_specs=[hbm] * 8,
-        out_specs=(vmem,) * 6,
+        in_specs=[hbm] * 5,
+        out_specs=(vmem,) * 4,
         scratch_shapes=[
             pltpu.VMEM((2, SIDE) + block, bf16),
             pltpu.VMEM((2, SIDE) + block, bf16),
@@ -365,34 +380,21 @@
             pltpu.VMEM((2,) + block, f32),
             pltpu.VMEM((2, SIDE - 1, HALF, COLS), bf16),
             pltpu.VMEM((2, SIDE - 1, HALF, COLS), bf16),
-            pltpu.VMEM(grid, bf16),
-            pltpu.VMEM((3, PANEL, ORDER), f32),
             pltpu.VMEM((3, PANEL, ORDER), bf16),
-            pltpu.VMEM((16, QC), f32),
-            pltpu.VMEM((2, KC, KC), f32),
             pltpu.VMEM((QC, QC), bf16),
             pltpu.VMEM((2, KC, KC), bf16),
             pltpu.VMEM((PANEL, COLS), f32),
             pltpu.VMEM((2 * KC, 2 * KC), bf16),
-            pltpu.VMEM((128, QC), f32),
             pltpu.VMEM((4, 8, 128), f32),
             pltpu.VMEM((5 * SIDE, 8, 128), f32),
             pltpu.SemaphoreType.DMA((10,)),
             pltpu.SemaphoreType.DMA((28,)),
-            pltpu.SemaphoreType.DMA((9,)),
+            pltpu.SemaphoreType.DMA((6,)),
         ],
         compiler_params=pltpu.CompilerParams(
             collective_id=0, has_side_effects=True, vmem_limit_bytes=40 * 1024 * 1024
         ),
-    )(
-        *(
-            pltpu.with_memory_space_constraint(array, pltpu.HBM)
-            for array in (
-                grads.reshape(grid), left_factor[0], left_root[0], right_q[0], right_kv[0],
-                right_q_root[0], right_kv_root[0], moment,
-            )
-        )
-    )
+    )(*stay(grads.reshape(grid), left_root[0], right_q_root[0], right_kv_root[0], moment))
     direction, left_new, rq_new, rkv_new, mom_new = pl.pallas_call(
         finish,
         out_shape=(
@@ -402,14 +404,18 @@
             shape((2, KC, KC), f32),
             shape((PANEL, COLS), f32),
         ),
-        in_specs=[vmem] * 6,
+        in_specs=[vmem] * 4 + [hbm] * 3,
         out_specs=(hbm,) * 5,
         scratch_shapes=[
             pltpu.VMEM((SIDE, ORDER // SIDE, COLS), bf16),
-            pltpu.SemaphoreType.DMA((4 + SIDE,)),
+            pltpu.VMEM((3, PANEL, ORDER), f32),
+            pltpu.VMEM((16, QC), f32),
+            pltpu.VMEM((2, KC, KC), f32),
+            pltpu.VMEM((128, QC), f32),
+            pltpu.SemaphoreType.DMA((11,)),
         ],
         compiler_params=pltpu.CompilerParams(vmem_limit_bytes=40 * 1024 * 1024),
-    )(gathered, scale_row, left_new, rq_new, rkv_new, mom_new)
+    )(gathered, total, scale_row, mom_new, *stay(left_factor[0], right_q[0], right_kv[0]))
     return direction, left_new[None], rq_new[None], rkv_new[None], mom_new
 
 

time: 57.7 us -> 59.2 us (1.026)
  Pallas kernels: 56.8 us -> 58.3 us
    pallas_call x1, Pallas kernels: 1.31 us -> 2.89 us  [local_step(): pl.pallas_call(finish, out_shape=(shape((ORDER, COLS), bf16), shape((3, P...]
where the time goes in v3:
time: 59.2 us; the launch traced here: 59 us
  Pallas kernels  58.3 us (98%)
  between operations  0.64 us (1%)
    pallas_call x1, Pallas kernels, local_step(): pl.pallas_call(kernel, out_shape=(shape(grid, bf16), shape(grid, bf16), s...  55.4 us
    pallas_call x1, Pallas kernels, local_step(): pl.pallas_call(finish, out_shape=(shape((ORDER, COLS), bf16), shape((3, P...  2.89 us

profile of v3, /device:TPU:1, one launch (start us, length us, event | category | flops | bytes accessed | tf_op | source)
XLA Modules:
  0.0 59.0 jit_solution(14652411766214039808)
XLA Ops:
  0.6 55.4 %shard_map.119 = (bf16[4,4,2,2,16,640]{5,4,3,2,1,0:T(8,128)(2,1)S(1)}, bf16[4,4,2,2,16,640]{5,4,3,2,1,0:T(8,128)(2,1)S(1)}, f32[8,640]{1,0:T(8,128)S(1)}, f32[32,640]{1,0:T(8,128)S(1)}) custom-call(bf16[4,4,2,2,16,640]{5,4,3,2,1,0:T(8,128)(2,1)} %bitcast.10, bf16[3,32,1024]{2,1,0:T(8,128)(2,1)} %bitcast.13, bf16[512,512]{1,0:T(8,128)(2,1)} %bitcast.11, ...), custom_call_target="tpu_custom_call" | custom-call | tf_op jit(solution)/shard_map/pallas_call | solution.py:365
  56.1 2.9 %shard_map.120 = (bf16[1024,640]{1,0:T(8,128)(2,1)}, f32[3,32,1024]{2,1,0:T(8,128)}, f32[16,512]{1,0:T(8,128)}, f32[2,64,64]{2,1,0:T(8,128)}, f32[32,640]{1,0:T(8,128)}) custom-call(bf16[4,4,2,2,16,640]{5,4,3,2,1,0:T(8,128)(2,1)S(1)} %get-tuple-element.14.gathered, bf16[4,4,2,2,16,640]{5,4,3,2,1,0:T(8,128)(2,1)S(1)} %get-tuple-element.15.total, ...), custom_call_target="tpu_custom_call" | custom-call | tf_op jit(solution)/shard_map/pallas_call | solution.py:398

commit v4 on v2

--- a/solution.py
+++ b/solution.py
@@ -44,11 +44,12 @@
     other = 1 - core
     y = lax.rem(dp // 2, SIDE)
     x = dp // (2 * SIDE)
-    z_low = lax.rem(z, SIDE)
-    z_high = z // SIDE
-
-    def at(i, j, k):
-        return ((i * SIDE + j) * 2 + k, z)
+    z_low = lax.rem(z, 2)
+    z_high = z // 2
+    deep = lax.axis_size("mp") // 2
+
+    def at(i, j, k, depth=z):
+        return ((i * SIDE + j) * 2 + k, depth)
 
     def ring(v):
         return [v] + [lax.rem(v + k, SIDE) for k in range(1, SIDE)]
@@ -61,11 +62,11 @@
     first = (on_x, on_y)
     second = (on_y, on_x)
     crossed = [at(x, ys[k], other) for k in others]
-    on_low = [(dp, z_high * SIDE + v) for v in ring(z_low)[1:]]
-    on_high = [(dp, v * SIDE + z_low) for v in ring(z_high)[1:]]
+    slanted = [at(v, y, core, 2 * z_high + 1 - z_low) for v in xs]
+    on_high = [(dp, 2 * lax.rem(z_high + k, deep) + z_low) for k in range(1, deep)]
 
     barrier = pltpu.get_barrier_semaphore()
-    partners = [sibling] + on_x[1:] + on_y[1:] + crossed + on_low + on_high
+    partners = [sibling] + on_x[1:] + on_y[1:] + crossed + slanted + on_high
     for device in partners:
         pl.semaphore_signal(barrier, inc=1, device_id=device, device_id_type=MESH)
 
@@ -77,7 +78,11 @@
         local.append(copy)
         return copy
 
-    mine = [load(g.at[:, :, core, h], own.at[h]) for h in range(2)]
+    def group(ref, h, k, c):
+        return ref.at[xs[k], :, c, 0] if h == 0 else ref.at[:, ys[k], c, 1]
+
+    far_first = FAR_FIRST + (0,)
+    mine = {(h, k): load(group(g, h, k, core), own.at[h, k]) for k in far_first for h in range(2)}
     pl.semaphore_wait(barrier, len(partners))
 
     sends = {}
@@ -103,11 +108,9 @@
         else:
             copy.wait_recv()
 
-    def group(ref, h, k, c):
-        return ref.at[xs[k], :, c, 0] if h == 0 else ref.at[:, ys[k], c, 1]
-
-    for h in range(2):
-        send(g.at[:, :, other, h], sib.at[h], sibling, "pair", ("pair", h))
+    for k in far_first:
+        for h in range(2):
+            send(group(g, h, k, other), sib.at[h, k], sibling, "pair", ("pair", h, k))
 
     mom_load = load(mom, mom_v)
     lr_load = load(lr, lr_v)
@@ -115,19 +118,16 @@
     rkvr_load = load(rkvr, rkvr_v)
     rest = [load(lf, lf_v), load(rq, rq_v), load(rkv, rkv_v)]
 
-    for h in range(2):
-        mine[h].wait()
-        all_of(sib.at[h], incoming=("pair", h))
-
-        def pair_sum(k):
-            if h == 0:
-                return own[h, xs[k]].astype(f32) + sib[h, xs[k]].astype(f32)
-            return own[h, :, ys[k]].astype(f32) + sib[h, :, ys[k]].astype(f32)
-
-        for k in FAR_FIRST:
-            part[h, k - 1] = pair_sum(k).astype(bf16)
-            send(part.at[h, k - 1], recv1.at[h, k - 1], first[h][k], "step1", ("step1", h))
-        acc[h] = pair_sum(0)
+    for k in far_first:
+        for h in range(2):
+            mine[h, k].wait()
+            all_of(sib.at[h, k], incoming=("pair", h, k))
+            pair_sum = own[h, k].astype(f32) + sib[h, k].astype(f32)
+            if k:
+                part[h, k - 1] = pair_sum.astype(bf16)
+                send(part.at[h, k - 1], recv1.at[h, k - 1], first[h][k], "step1", ("step1", h))
+            else:
+                acc[h] = pair_sum
 
     kept = []
     for h in range(2):
@@ -222,44 +222,44 @@
     proj_kv = jnp.where(is_key, both[:PANEL], both[PANEL:]).astype(bf16)
     cond_q = dot(proj_q, rqr_v[...])
     cond_kv = dot(proj_kv, diag[...])
+
+    eight = 2 * SIDE
+    levels = (
+        (2 * y + core, on_y[1:] + [sibling] + crossed),
+        (2 * x + z_low, on_x[1:] + slanted),
+        (z_high, on_high),
+    )
+
+    def norm_send(level):
+        place, devices = levels[level]
+        slot = level * eight + place
+        norm_in[slot] = norm[level]
+        for device in devices:
+            send(norm.at[level], norm_in.at[slot], device, "norm", ("norm", level))
+
+    def norm_add(level):
+        start = level * eight
+        all_of(norm_in.at[start : start + eight - 1], incoming=("norm", level))
+        value = norm_in[start]
+        for i in range(1, eight):
+            value = value + norm_in[start + i]
+        return value
+
+    def norm_step(level):
+        norm[level] = norm_add(level - 1)
+        norm_send(level)
+
+    square = jnp.square(jnp.concatenate([cond_q, cond_kv], axis=1))
+    cond_lanes_q, cond_lanes_kv = to_lanes(square)
+    norm[0, 2:3, :] = cond_lanes_q
+    norm[0, 3:4, :] = cond_lanes_kv
+    norm_send(0)
     gathered[x, y, core, :, :, :QC] = cond_q.astype(bf16).reshape(2, HALF, QC)
     gathered[x, y, core, :, :, QC:] = cond_kv.astype(bf16).reshape(2, HALF, 2 * KC)
     for h in range(2):
         for k in FAR_FIRST:
             block = gathered.at[x, y, core, h]
             send(block, block, second[h][k], "across1", ("across1", h))
-
-    levels = (
-        (0, 2 * SIDE, 2 * y + core, on_y[1:] + [sibling] + crossed),
-        (2 * SIDE, SIDE, x, on_x[1:]),
-        (3 * SIDE, SIDE, z_low, on_low),
-        (4 * SIDE, SIDE, z_high, on_high),
-    )
-
-    def norm_send(level):
-        start, _, place, devices = levels[level]
-        norm_in[start + place] = norm[level]
-        for device in devices:
-            send(norm.at[level], norm_in.at[start + place], device, "norm", ("norm", level))
-
-    def norm_add(level):
-        start, count, _, _ = levels[level]
-        all_of(norm_in.at[start : start + count - 1], incoming=("norm", level))
-        value = norm_in[start]
-        for i in range(1, count):
-            value = value + norm_in[start + i]
-        return value
-
-    def norm_step(level):
-        norm[level] = norm_add(level - 1)
-        norm_send(level)
-
-    def norm_start():
-        square = jnp.square(jnp.concatenate([cond_q, cond_kv], axis=1))
-        cond_lanes_q, cond_lanes_kv = to_lanes(square)
-        norm[0, 2:3, :] = cond_lanes_q
-        norm[0, 3:4, :] = cond_lanes_kv
-        norm_send(0)
 
     def left_part():
         owned = total[x, y, core].reshape(PANEL, COLS)
@@ -282,15 +282,17 @@
         moved = pltpu.roll(square, KC, 1)
         rkv_new[1] = factor_keep * rkv_v[1] + factor_add * moved[KC:, :KC]
 
-    def middle_part():
+    def early_part():
+        left_part()
         norm_step(1)
-        left_part()
+        right_part()
         norm_step(2)
-        right_part()
-        norm_step(3)
+
+    def wait_rest():
+        pass
 
     def scale_part():
-        sums = norm_add(3)
+        sums = norm_add(2)
 
         def whole(row_index, mask):
             values = sums[row_index : row_index + 1, :]
@@ -307,7 +309,7 @@
         scale_row[:, :QC] = jnp.broadcast_to(scale_q, (8, QC))
         scale_row[:, QC:] = jnp.broadcast_to(jnp.where(is_key, scale_k, scale_v), (8, 2 * KC))
 
-    gather(gathered, "1", norm_start, middle_part, scale_part)
+    gather(gathered, "1", early_part, wait_rest, scale_part)
 
     all_of(sib, outgoing="pair")
     all_of(recv1, outgoing="step1")
@@ -316,7 +318,7 @@
         all_of(recv2, outgoing="across" + name)
         all_of(recv1, outgoing="along" + name)
         all_of(ref.at[:, :, core], outgoing="over" + name)
-    all_of(norm_in.at[: 4 * SIDE], outgoing="norm")
+    all_of(norm_in.at[: 3 * (eight - 1)], outgoing="norm")
     assert len(sends) == ssem.shape[0] and len(arrivals) == rsem.shape[0]
 
 
@@ -375,11 +377,11 @@
             pltpu.VMEM((PANEL, COLS), f32),
             pltpu.VMEM((2 * KC, 2 * KC), bf16),
             pltpu.VMEM((128, QC), f32),
-            pltpu.VMEM((4, 8, 128), f32),
-            pltpu.VMEM((5 * SIDE, 8, 128), f32),
+            pltpu.VMEM((3, 8, 128), f32),
+            pltpu.VMEM((6 * SIDE, 8, 128), f32),
             pltpu.SemaphoreType.DMA((10,)),
-            pltpu.SemaphoreType.DMA((28,)),
-            pltpu.SemaphoreType.DMA((9,)),
+            pltpu.SemaphoreType.DMA((33,)),
+            pltpu.SemaphoreType.DMA((15,)),
         ],
         compiler_params=pltpu.CompilerParams(
             collective_id=0, has_side_effects=True, vmem_limit_bytes=40 * 1024 * 1024

time: 57.7 us -> 55.8 us (0.967)
  Pallas kernels: 56.8 us -> 55.1 us
    pallas_call x1, Pallas kernels: 55.5 us -> 53.8 us  [local_step(): pl.pallas_call(kernel, out_shape=(shape(grid, bf16), shape((8, COLS), f32...]
where the time goes in v4:
time: 55.8 us; the launch traced here: 55.7 us
  Pallas kernels  55.1 us (99%)
  between operations  0.64 us (1%)
    pallas_call x1, Pallas kernels, local_step(): pl.pallas_call(kernel, out_shape=(shape(grid, bf16), shape((8, COLS), f32...  53.8 us
    pallas_call x1, Pallas kernels, local_step(): pl.pallas_call(finish, out_shape=(shape((ORDER, COLS), bf16), shape((3, P...  1.31 us

profile of v4, /device:TPU:1, one launch (start us, length us, event | category | flops | bytes accessed | tf_op | source)
XLA Modules:
  0.0 55.7 jit_solution(9769063823281102627)
XLA Ops:
  0.6 53.8 %shard_map.119 = (bf16[4,4,2,2,16,640]{5,4,3,2,1,0:T(8,128)(2,1)S(1)}, f32[8,640]{1,0:T(8,128)S(1)}, f32[3,32,1024]{2,1,0:T(8,128)S(1)}, f32[16,512]{1,0:T(8,128...) custom-call(bf16[4,4,2,2,16,640]{5,4,3,2,1,0:T(8,128)(2,1)} %bitcast.10, f32[3,32,1024]{2,1,0:T(8,128)} %bitcast.12, ...), custom_call_target="tpu_custom_call" | custom-call | tf_op jit(solution)/shard_map/pallas_call | solution.py:350
  54.4 1.3 %shard_map.120 = (bf16[1024,640]{1,0:T(8,128)(2,1)}, f32[3,32,1024]{2,1,0:T(8,128)}, f32[16,512]{1,0:T(8,128)}, f32[2,64,64]{2,1,0:T(8,128)}, f32[32,640]{1,0:T(8,128)}) custom-call(bf16[4,4,2,2,16,640]{5,4,3,2,1,0:T(8,128)(2,1)S(1)} %get-tuple-element.16.gathered, f32[8,640]{1,0:T(8,128)S(1)} %get-tuple-element.17.scale_row, ...), custom_call_target="tpu_custom_call" | custom-call | tf_op jit(solution)/shard_map/pallas_call | solution.py:398

commit v5 on v4

--- a/solution.py
+++ b/solution.py
@@ -23,11 +23,21 @@
 COLS = QC + 2 * KC
 ORDER = 1024
 PANEL = 32
-FAR_FIRST = (2, 1, 3)
+FLIPS = ((1, 1), (1, 0), (0, 1))
 
 
 def dot(a, b, ca=1, cb=0):
     return lax.dot_general(a, b, (((ca,), (cb,)), ((), ())), preferred_element_type=f32)
+
+
+def in_order(ref, cols, lines=range(SIDE)):
+    return jnp.concatenate(
+        [
+            ref[h, (i + 1 - h) % SIDE, (j + 1 - h) % SIDE, k, :, cols]
+            for i in lines for j in range(SIDE) for k in range(2) for h in range(2)
+        ],
+        axis=0,
+    )
 
 
 def kernel(
@@ -44,29 +54,35 @@
     other = 1 - core
     y = lax.rem(dp // 2, SIDE)
     x = dp // (2 * SIDE)
-    z_low = lax.rem(z, 2)
-    z_high = z // 2
-    deep = lax.axis_size("mp") // 2
-
-    def at(i, j, k, depth=z):
-        return ((i * SIDE + j) * 2 + k, depth)
-
-    def ring(v):
-        return [v] + [lax.rem(v + k, SIDE) for k in range(1, SIDE)]
+    depth = lax.axis_size("mp")
+
+    def at(i, j, k):
+        return ((i * SIDE + j) * 2 + k, z)
 
     sibling = at(x, y, other)
-    xs, ys = ring(x), ring(y)
-    others = range(1, SIDE)
-    on_x = [None] + [at(xs[k], y, core) for k in others]
-    on_y = [None] + [at(x, ys[k], core) for k in others]
-    first = (on_x, on_y)
-    second = (on_y, on_x)
-    crossed = [at(x, ys[k], other) for k in others]
-    slanted = [at(v, y, core, 2 * z_high + 1 - z_low) for v in xs]
-    on_high = [(dp, 2 * lax.rem(z_high + k, deep) + z_low) for k in range(1, deep)]
+    halves = range(2)
+    u = [lax.rem(x + 1, SIDE), x]
+    v = [lax.rem(y + 1, SIDE), y]
+
+    def near(place):
+        odd = lax.rem(place, 2)
+        return place + 1 - 2 * odd, lax.rem(place + SIDE - 1 + 2 * odd, SIDE)
+
+    def back(h, place):
+        return lax.rem(place + SIDE - 1 + h, SIDE)
+
+    def quad(h, kind, k):
+        i = (x, back(h, near(u[h])[kind]))
+        j = (y, back(h, near(v[h])[kind]))
+        return [at(i[a], j[b], k) for a, b in FLIPS]
+
+    small = [quad(h, 0, core) for h in halves]
+    large = [quad(h, 1, core) for h in halves]
+    crossed = quad(0, 1, other)
+    on_z = [(dp, lax.rem(z + k, depth)) for k in range(1, depth)]
 
     barrier = pltpu.get_barrier_semaphore()
-    partners = [sibling] + on_x[1:] + on_y[1:] + crossed + slanted + on_high
+    partners = [sibling] + large[0] + large[1] + crossed + on_z
     for device in partners:
         pl.semaphore_signal(barrier, inc=1, device_id=device, device_id_type=MESH)
 
@@ -78,11 +94,13 @@
         local.append(copy)
         return copy
 
-    def group(ref, h, k, c):
-        return ref.at[xs[k], :, c, 0] if h == 0 else ref.at[:, ys[k], c, 1]
-
-    far_first = FAR_FIRST + (0,)
-    mine = {(h, k): load(group(g, h, k, core), own.at[h, k]) for k in far_first for h in range(2)}
+    pair_u = [u[h] // 2 for h in halves]
+    pair_v = [v[h] // 2 for h in halves]
+    lines = [
+        [back(h, 2 * (1 - pair_u[h])), back(h, 3 - 2 * pair_u[h]), back(h, 2 * pair_u[h]), back(h, 2 * pair_u[h] + 1)]
+        for h in halves
+    ]
+    mine = {(h, i): load(g.at[lines[h][i], :, core, h], own.at[h, i]) for i in range(SIDE) for h in halves}
     pl.semaphore_wait(barrier, len(partners))
 
     sends = {}
@@ -108,9 +126,9 @@
         else:
             copy.wait_recv()
 
-    for k in far_first:
-        for h in range(2):
-            send(group(g, h, k, other), sib.at[h, k], sibling, "pair", ("pair", h, k))
+    for i in range(SIDE):
+        for h in halves:
+            send(g.at[lines[h][i], :, other, h], sib.at[h, i], sibling, "pair", ("pair", h, i))
 
     mom_load = load(mom, mom_v)
     lr_load = load(lr, lr_v)
@@ -118,61 +136,85 @@
     rkvr_load = load(rkvr, rkvr_v)
     rest = [load(lf, lf_v), load(rq, rq_v), load(rkv, rkv_v)]
 
-    for k in far_first:
-        for h in range(2):
-            mine[h, k].wait()
-            all_of(sib.at[h, k], incoming=("pair", h, k))
-            pair_sum = own[h, k].astype(f32) + sib[h, k].astype(f32)
-            if k:
-                part[h, k - 1] = pair_sum.astype(bf16)
-                send(part.at[h, k - 1], recv1.at[h, k - 1], first[h][k], "step1", ("step1", h))
-            else:
-                acc[h] = pair_sum
+    def pair_sum(h, a, flip_u, flip_v, b):
+        i = a if flip_u else 2 + a
+        pair = 1 - pair_v[h] if flip_v else pair_v[h]
+        j = back(h, 2 * pair + b)
+        return own[h, i, j].astype(f32) + sib[h, i, j].astype(f32)
+
+    for flip_u in (1, 0):
+        for h in halves:
+            for i in (0, 1) if flip_u else (2, 3):
+                mine[h, i].wait()
+                all_of(sib.at[h, i], incoming=("pair", h, i))
+            for flip_v in (1, 0):
+                for a in range(2):
+                    for b in range(2):
+                        value = pair_sum(h, a, flip_u, flip_v, b)
+                        if flip_u or flip_v:
+                            part[h, FLIPS.index((flip_u, flip_v)), a, b] = value.astype(bf16)
+                        else:
+                            acc[h, a, b] = value
+                if flip_u or flip_v:
+                    i = FLIPS.index((flip_u, flip_v))
+                    send(part.at[h, i], recv1.at[h, i], large[h][i], "step1", ("step1", h))
+
+    odd_u = [lax.rem(u[h], 2) for h in halves]
+    odd_v = [lax.rem(v[h], 2) for h in halves]
+
+    def quad_sum(h, flip_u, flip_v):
+        a = 1 - odd_u[h] if flip_u else odd_u[h]
+        b = 1 - odd_v[h] if flip_v else odd_v[h]
+        value = acc[h, a, b]
+        for i in range(3):
+            value = value + recv1[h, i, a, b].astype(f32)
+        return value
 
     kept = []
-    for h in range(2):
+    for h in halves:
         all_of(recv1.at[h], incoming=("step1", h))
-
-        def line_sum(k):
-            j = (ys if h == 0 else xs)[k]
-            value = acc[h, j]
-            for i in range(SIDE - 1):
-                value = value + recv1[h, i, j].astype(f32)
-            return value
-
-        for k in FAR_FIRST:
-            part2[h, k - 1] = line_sum(k).astype(bf16)
-            send(part2.at[h, k - 1], recv2.at[h, k - 1], second[h][k], "step2", ("step2", h))
-        kept.append(line_sum(0))
+        for i in range(3):
+            part2[h, i] = quad_sum(h, *FLIPS[i]).astype(bf16)
+            send(part2.at[h, i], recv2.at[h, i], small[h][i], "step2", ("step2", h))
+        kept.append(quad_sum(h, 0, 0))
     three = recv2.at[0]
-    for h in range(2):
+
+    def across(ref, name, h):
+        block = ref.at[h, u[h], v[h], core]
+        for i in range(3):
+            send(block, block, small[h][i], "across" + name, ("across" + name, h))
+
+    for h in halves:
         value = kept[h]
         all_of(recv2.at[h], incoming=("step2", h))
-        for i in range(SIDE - 1):
+        for i in range(3):
             value = value + recv2[h, i].astype(f32)
-        total[x, y, core, h] = value.astype(bf16)
-        for k in FAR_FIRST:
-            block = total.at[x, y, core, h]
-            send(block, block, second[h][k], "across0", ("across0", h))
+        total[h, u[h], v[h], core] = value.astype(bf16)
+        across(total, "0", h)
+
+    def group(ref, h, flip_u, flip_v):
+        i = 1 - pair_u[h] if flip_u else pair_u[h]
+        j = 1 - pair_v[h] if flip_v else pair_v[h]
+        return ref.at[h, pl.ds(2 * i, 2), pl.ds(2 * j, 2), core]
 
     def gather(ref, name, early, middle, late):
         early()
-        for h in range(2):
+        for h in halves:
             all_of(three, incoming=("across" + name, h))
-            block = group(ref, h, 0, core)
-            for k in FAR_FIRST:
-                send(block, block, first[h][k], "along" + name, ("along" + name, h, k))
-        for h in range(2):
-            block = group(ref, h, 0, core)
+            block = group(ref, h, 0, 0)
+            for i in range(3):
+                send(block, block, large[h][i], "along" + name, ("along" + name, h, i))
+        for h in halves:
+            block = group(ref, h, 0, 0)
             send(block, block, sibling, "over" + name, "over" + name)
         middle()
-        for k in (1, 3, 2):
-            for h in range(2):
-                block = group(ref, h, SIDE - k, core)
-                all_of(block, incoming=("along" + name, h, k))
+        for i in (1, 2, 0):
+            for h in halves:
+                block = group(ref, h, *FLIPS[i])
+                all_of(block, incoming=("along" + name, h, i))
                 send(block, block, sibling, "over" + name, "over" + name)
         late()
-        all_of(ref.at[:, :, other], incoming="over" + name)
+        all_of(ref.at[:, :, :, other], incoming="over" + name)
 
     lane = lax.broadcasted_iota(jnp.int32, (1, 2 * KC), 1)
     is_key = lane < KC
@@ -184,9 +226,12 @@
             query = query + column[:, 128 * i : 128 * (i + 1)]
         return query, column[:, QC:]
 
+    def my_rows():
+        return jnp.concatenate([total[h, u[h], v[h], core] for h in halves], axis=0)
+
     def graft_part():
         mom_load.wait()
-        row_grad = total[x, y, core].reshape(PANEL, COLS).astype(f32)
+        row_grad = my_rows().astype(f32)
         moment_new = moment_keep * mom_v[...] + moment_add * row_grad * row_grad
         mom_new[...] = moment_new
         graft = row_grad / (jnp.sqrt(moment_new) + graft_eps)
@@ -212,10 +257,10 @@
     gather(total, "0", graft_part, diagonal_part, wait_loads)
 
     def query_grad():
-        return total[..., :QC].reshape(ORDER, QC)
+        return in_order(total, slice(0, QC))
 
     def key_value_grad():
-        return total[..., QC:].reshape(ORDER, 2 * KC)
+        return in_order(total, slice(QC, COLS))
 
     proj_q = dot(lr_v[0], query_grad()).astype(bf16)
     both = dot(lr_v[1:3].reshape(2 * PANEL, ORDER), key_value_grad())
@@ -223,25 +268,23 @@
     cond_q = dot(proj_q, rqr_v[...])
     cond_kv = dot(proj_kv, diag[...])
 
-    eight = 2 * SIDE
     levels = (
-        (2 * y + core, on_y[1:] + [sibling] + crossed),
-        (2 * x + z_low, on_x[1:] + slanted),
-        (z_high, on_high),
+        (0, 8, 4 * lax.rem(x, 2) + 2 * lax.rem(y, 2) + core, large[0] + [sibling] + crossed),
+        (8, 4, 2 * odd_u[0] + odd_v[0], large[1]),
+        (12, depth, z, on_z),
     )
 
     def norm_send(level):
-        place, devices = levels[level]
-        slot = level * eight + place
-        norm_in[slot] = norm[level]
+        start, _, place, devices = levels[level]
+        norm_in[start + place] = norm[level]
         for device in devices:
-            send(norm.at[level], norm_in.at[slot], device, "norm", ("norm", level))
+            send(norm.at[level], norm_in.at[start + place], device, "norm", ("norm", level))
 
     def norm_add(level):
-        start = level * eight
-        all_of(norm_in.at[start : start + eight - 1], incoming=("norm", level))
+        start, count, _, _ = levels[level]
+        all_of(norm_in.at[start : start + count - 1], incoming=("norm", level))
         value = norm_in[start]
-        for i in range(1, eight):
+        for i in range(1, count):
             value = value + norm_in[start + i]
         return value
 
@@ -254,15 +297,14 @@
     norm[0, 2:3, :] = cond_lanes_q
     norm[0, 3:4, :] = cond_lanes_kv
     norm_send(0)
-    gathered[x, y, core, :, :, :QC] = cond_q.astype(bf16).reshape(2, HALF, QC)
-    gathered[x, y, core, :, :, QC:] = cond_kv.astype(bf16).reshape(2, HALF, 2 * KC)
-    for h in range(2):
-        for k in FAR_FIRST:
-            block = gathered.at[x, y, core, h]
-            send(block, block, second[h][k], "across1", ("across1", h))
+    for h in halves:
+        rows = slice(HALF * h, HALF * (h + 1))
+        gathered[h, u[h], v[h], core, :, :QC] = cond_q[rows].astype(bf16)
+        gathered[h, u[h], v[h], core, :, QC:] = cond_kv[rows].astype(bf16)
+        across(gathered, "1", h)
 
     def left_part():
-        owned = total[x, y, core].reshape(PANEL, COLS)
+        owned = my_rows()
         owned_kv = owned[:, QC:].astype(f32)
         split = jnp.concatenate(
             [jnp.where(is_key, owned_kv, 0.0), jnp.where(is_key, 0.0, owned_kv)], axis=0
@@ -274,10 +316,13 @@
 
     def right_part():
         columns = pl.ds(pl.multiple_of(x * 128, 128), 128)
-        slab[...] = dot(total[..., columns].reshape(ORDER, 128), query_grad(), 0, 0)
+        slab[...] = dot(
+            total[..., columns].reshape(ORDER, 128), total[..., :QC].reshape(ORDER, QC), 0, 0
+        )
         mine_q = pl.ds(pl.multiple_of(lax.rem(dp, 2 * SIDE) * 16, 16), 16)
         rq_new[...] = factor_keep * rq_v[...] + factor_add * slab[mine_q, :]
-        square = dot(key_value_grad(), key_value_grad(), 0, 0)
+        key_value = total[..., QC:].reshape(ORDER, 2 * KC)
+        square = dot(key_value, key_value, 0, 0)
         rkv_new[0] = factor_keep * rkv_v[0] + factor_add * square[:KC, :KC]
         moved = pltpu.roll(square, KC, 1)
         rkv_new[1] = factor_keep * rkv_v[1] + factor_add * moved[KC:, :KC]
@@ -317,8 +362,8 @@
     for name, ref in (("0", total), ("1", gathered)):
         all_of(recv2, outgoing="across" + name)
         all_of(recv1, outgoing="along" + name)
-        all_of(ref.at[:, :, core], outgoing="over" + name)
-    all_of(norm_in.at[: 3 * (eight - 1)], outgoing="norm")
+        all_of(ref.at[:, :, :, core], outgoing="over" + name)
+    all_of(norm_in.at[: 7 + 3 + depth - 1], outgoing="norm")
     assert len(sends) == ssem.shape[0] and len(arrivals) == rsem.shape[0]
 
 
@@ -335,7 +380,7 @@
     height = ORDER // SIDE
     scale = scale_row[0:1, :]
     for i in range(SIDE):
-        rows[i] = (gathered[i].reshape(height, COLS).astype(f32) * scale).astype(bf16)
+        rows[i] = (in_order(gathered, slice(0, COLS), (i,)).astype(f32) * scale).astype(bf16)
         store(rows.at[i], direction.at[pl.ds(i * height, height)])
     for copy in copies:
         copy.wait()
@@ -343,6 +388,9 @@
 
 def local_step(grads, left_factor, left_root, right_q, right_kv, right_q_root, right_kv_root, moment):
     grid = (SIDE, SIDE, 2, 2, HALF, COLS)
+    by_half = (2, SIDE, SIDE, 2, HALF, COLS)
+    depth = lax.axis_size("mp")
+    quad_block = (2, 2, HALF, COLS)
     block = (SIDE, HALF, COLS)
     hbm = pl.BlockSpec(memory_space=pltpu.HBM)
     vmem = pl.BlockSpec(memory_space=pltpu.VMEM)
@@ -350,7 +398,7 @@
     gathered, scale_row, left_new, rq_new, rkv_new, mom_new = pl.pallas_call(
         kernel,
         out_shape=(
-            shape(grid, bf16),
+            shape(by_half, bf16),
             shape((8, COLS), f32),
             shape((3, PANEL, ORDER), f32),
             shape((16, QC), f32),
@@ -362,12 +410,12 @@
         scratch_shapes=[
             pltpu.VMEM((2, SIDE) + block, bf16),
             pltpu.VMEM((2, SIDE) + block, bf16),
-            pltpu.VMEM((2, SIDE - 1) + block, bf16),
-            pltpu.VMEM((2, SIDE - 1) + block, bf16),
-            pltpu.VMEM((2,) + block, f32),
+            pltpu.VMEM((2, 3) + quad_block, bf16),
+            pltpu.VMEM((2, 3) + quad_block, bf16),
+            pltpu.VMEM((2,) + quad_block, f32),
             pltpu.VMEM((2, SIDE - 1, HALF, COLS), bf16),
             pltpu.VMEM((2, SIDE - 1, HALF, COLS), bf16),
-            pltpu.VMEM(grid, bf16),
+            pltpu.VMEM(by_half, bf16),
             pltpu.VMEM((3, PANEL, ORDER), f32),
             pltpu.VMEM((3, PANEL, ORDER), bf16),
             pltpu.VMEM((16, QC), f32),
@@ -378,7 +426,7 @@
             pltpu.VMEM((2 * KC, 2 * KC), bf16),
             pltpu.VMEM((128, QC), f32),
             pltpu.VMEM((3, 8, 128), f32),
-            pltpu.VMEM((6 * SIDE, 8, 128), f32),
+            pltpu.VMEM((12 + depth, 8, 128), f32),
             pltpu.SemaphoreType.DMA((10,)),
             pltpu.SemaphoreType.DMA((33,)),
             pltpu.SemaphoreType.DMA((15,)),

time: 55.8 us -> 56 us (level)
  no operation moved by 1% of the time
where the time goes in v5:
time: 56 us; the launch traced here: 55.9 us
  Pallas kernels  55.3 us (99%)
  between operations  0.64 us (1%)
    pallas_call x1, Pallas kernels, local_step(): pl.pallas_call(kernel, out_shape=(shape(by_half, bf16), shape((8, COLS),...  54 us
    pallas_call x1, Pallas kernels, local_step(): pl.pallas_call(finish, out_shape=(shape((ORDER, COLS), bf16), shape((3, P...  1.31 us

profile of v5, /device:TPU:1, one launch (start us, length us, event | category | flops | bytes accessed | tf_op | source)
XLA Modules:
  0.0 55.9 jit_solution(13389554013420659001)
XLA Ops:
  0.6 54.0 %shard_map.119 = (bf16[2,4,4,2,16,640]{5,4,3,2,1,0:T(8,128)(2,1)S(1)}, f32[8,640]{1,0:T(8,128)S(1)}, f32[3,32,1024]{2,1,0:T(8,128)S(1)}, f32[16,512]{1,0:T(8,128...) custom-call(bf16[4,4,2,2,16,640]{5,4,3,2,1,0:T(8,128)(2,1)} %bitcast.10, f32[3,32,1024]{2,1,0:T(8,128)} %bitcast.12, ...), custom_call_target="tpu_custom_call" | custom-call | tf_op jit(solution)/shard_map/pallas_call | solution.py:398
  54.6 1.3 %shard_map.120 = (bf16[1024,640]{1,0:T(8,128)(2,1)}, f32[3,32,1024]{2,1,0:T(8,128)}, f32[16,512]{1,0:T(8,128)}, f32[2,64,64]{2,1,0:T(8,128)}, f32[32,640]{1,0:T(8,128)}) custom-call(bf16[2,4,4,2,16,640]{5,4,3,2,1,0:T(8,128)(2,1)S(1)} %get-tuple-element.16.gathered, f32[8,640]{1,0:T(8,128)S(1)} %get-tuple-element.17.scale_row, ...), custom_call_target="tpu_custom_call" | custom-call | tf_op jit(solution)/shard_map/pallas_call | solution.py:446

commit v6 on v5

--- a/solution.py
+++ b/solution.py
@@ -45,8 +45,8 @@
     gathered, scale_row, left_new, rq_new, rkv_new, mom_new,
     own, sib, part, recv1, acc, part2, recv2, total,
     lf_v, lr_v, rq_v, rkv_v, rqr_v, rkvr_v, mom_v,
-    diag, slab, norm, norm_in,
-    ssem, rsem, lsem,
+    roots_by, diag, slab, norm, norm_in,
+    ssem, rsem, lsem, known,
 ):
     dp = lax.axis_index("dp")
     z = lax.axis_index("mp")
@@ -79,10 +79,14 @@
     small = [quad(h, 0, core) for h in halves]
     large = [quad(h, 1, core) for h in halves]
     crossed = quad(0, 1, other)
-    on_z = [(dp, lax.rem(z + k, depth)) for k in range(1, depth)]
+    far_first = sorted(range(1, depth), key=lambda k: -min(k, depth - k))
+    on_z = [(dp, lax.rem(z + k, depth)) for k in far_first]
+
+    def beside(k):
+        return [(dp, lax.rem(z + k, depth)), (dp, lax.rem(z + depth - k, depth))]
 
     barrier = pltpu.get_barrier_semaphore()
-    partners = [sibling] + large[0] + large[1] + crossed + on_z
+    partners = [sibling] + large[0] + large[1] + crossed + beside(1)
     for device in partners:
         pl.semaphore_signal(barrier, inc=1, device_id=device, device_id_type=MESH)
 
@@ -102,6 +106,15 @@
     ]
     mine = {(h, i): load(g.at[lines[h][i], :, core, h], own.at[h, i]) for i in range(SIDE) for h in halves}
     pl.semaphore_wait(barrier, len(partners))
+
+    def tell(i):
+        for device in beside(2**i):
+            pl.semaphore_signal(known.at[i], inc=1, device_id=device, device_id_type=MESH)
+
+    def learn(i):
+        pl.semaphore_wait(known.at[i], 2)
+
+    tell(0)
 
     sends = {}
     arrivals = {}
@@ -158,6 +171,21 @@
                 if flip_u or flip_v:
                     i = FLIPS.index((flip_u, flip_v))
                     send(part.at[h, i], recv1.at[h, i], large[h][i], "step1", ("step1", h))
+
+    learn(0)
+    tell(1)
+
+    lr_load.wait()
+    roots = lr_v[...].reshape(3 * PANEL, ORDER)
+    column = lax.broadcasted_iota(jnp.int32, (1, ORDER // 2), 1)
+    half_of = column >> 8
+    u_of = ((column >> 6) + SIDE - 1 + half_of) & (SIDE - 1)
+    v_of = ((column >> 4) + SIDE - 1 + half_of) & (SIDE - 1)
+    wanted = u_of * 256 + v_of * 64 + half_of * HALF + (column & (HALF - 1))
+    row_of = lax.broadcasted_iota(jnp.int32, (ORDER, ORDER // 2), 0)
+    for i, parity in enumerate((core, other)):
+        chosen = jnp.where(row_of == wanted + parity * PANEL, 1.0, 0.0).astype(bf16)
+        roots_by[i] = dot(roots, chosen).astype(bf16)
 
     odd_u = [lax.rem(u[h], 2) for h in halves]
     odd_v = [lax.rem(v[h], 2) for h in halves]
@@ -248,13 +276,25 @@
             place = (col == row + i * KC).astype(f32).astype(bf16)
             diag[KC * i : KC * (i + 1), :] = dot(rkvr_v[i], place).astype(bf16)
 
+    saved = []
+
+    def project(i, parity):
+        rows_q = total[:, :, :, parity, :, :QC].reshape(ORDER // 2, QC)
+        rows_kv = total[:, :, :, parity, :, QC:].reshape(ORDER // 2, 2 * KC)
+        return dot(roots_by[i, :PANEL], rows_q), dot(roots_by[i, PANEL:], rows_kv)
+
     def wait_loads():
-        lr_load.wait()
         rqr_load.wait()
         for copy in rest:
             copy.wait()
-
-    gather(total, "0", graft_part, diagonal_part, wait_loads)
+        saved.append(project(0, core))
+
+    def middle_part():
+        diagonal_part()
+        learn(1)
+        tell(2)
+
+    gather(total, "0", graft_part, middle_part, wait_loads)
 
     def query_grad():
         return in_order(total, slice(0, QC))
@@ -262,8 +302,9 @@
     def key_value_grad():
         return in_order(total, slice(QC, COLS))
 
-    proj_q = dot(lr_v[0], query_grad()).astype(bf16)
-    both = dot(lr_v[1:3].reshape(2 * PANEL, ORDER), key_value_grad())
+    saved.append(project(1, other))
+    proj_q = (saved[0][0] + saved[1][0]).astype(bf16)
+    both = saved[0][1] + saved[1][1]
     proj_kv = jnp.where(is_key, both[:PANEL], both[PANEL:]).astype(bf16)
     cond_q = dot(proj_q, rqr_v[...])
     cond_kv = dot(proj_kv, diag[...])
@@ -331,6 +372,7 @@
         left_part()
         norm_step(1)
         right_part()
+        learn(2)
         norm_step(2)
 
     def wait_rest():
@@ -423,6 +465,7 @@
             pltpu.VMEM((QC, QC), bf16),
             pltpu.VMEM((2, KC, KC), bf16),
             pltpu.VMEM((PANEL, COLS), f32),
+            pltpu.VMEM((2, 3 * PANEL, ORDER // 2), bf16),
             pltpu.VMEM((2 * KC, 2 * KC), bf16),
             pltpu.VMEM((128, QC), f32),
             pltpu.VMEM((3, 8, 128), f32),
@@ -430,6 +473,7 @@
             pltpu.SemaphoreType.DMA((10,)),
             pltpu.SemaphoreType.DMA((33,)),
             pltpu.SemaphoreType.DMA((15,)),
+            pltpu.SemaphoreType.REGULAR((3,)),
         ],
         compiler_params=pltpu.CompilerParams(
             collective_id=0, has_side_effects=True, vmem_limit_bytes=40 * 1024 * 1024

time: 56 us -> 52 us (0.929)
  Pallas kernels: 55.3 us -> 51.2 us
    pallas_call x1, Pallas kernels: 54 us -> 49.9 us  [local_step(): pl.pallas_call(kernel, out_shape=(shape(by_half, bf16), shape((8, COLS),...]
where the time goes in v6:
time: 52 us; the launch traced here: 51.9 us
  Pallas kernels  51.2 us (98%)
  between operations  0.64 us (1%)
    pallas_call x1, Pallas kernels, local_step(): pl.pallas_call(kernel, out_shape=(shape(by_half, bf16), shape((8, COLS),...  49.9 us
    pallas_call x1, Pallas kernels, local_step(): pl.pallas_call(finish, out_shape=(shape((ORDER, COLS), bf16), shape((3, P...  1.31 us

profile of v6, /device:TPU:1, one launch (start us, length us, event | category | flops | bytes accessed | tf_op | source)
XLA Modules:
  0.0 51.9 jit_solution(17406366028792022979)
XLA Ops:
  0.6 49.9 %shard_map.119 = (bf16[2,4,4,2,16,640]{5,4,3,2,1,0:T(8,128)(2,1)S(1)}, f32[8,640]{1,0:T(8,128)S(1)}, f32[3,32,1024]{2,1,0:T(8,128)S(1)}, f32[16,512]{1,0:T(8,128...) custom-call(bf16[4,4,2,2,16,640]{5,4,3,2,1,0:T(8,128)(2,1)} %bitcast.10, f32[3,32,1024]{2,1,0:T(8,128)} %bitcast.12, ...), custom_call_target="tpu_custom_call" | custom-call | tf_op jit(solution)/shard_map/pallas_call | solution.py:440
  50.5 1.3 %shard_map.120 = (bf16[1024,640]{1,0:T(8,128)(2,1)}, f32[3,32,1024]{2,1,0:T(8,128)}, f32[16,512]{1,0:T(8,128)}, f32[2,64,64]{2,1,0:T(8,128)}, f32[32,640]{1,0:T(8,128)}) custom-call(bf16[2,4,4,2,16,640]{5,4,3,2,1,0:T(8,128)(2,1)S(1)} %get-tuple-element.16.gathered, f32[8,640]{1,0:T(8,128)S(1)} %get-tuple-element.17.scale_row, ...), custom_call_target="tpu_custom_call" | custom-call | tf_op jit(solution)/shard_map/pallas_call | solution.py:490

commit v7 on v6

--- a/solution.py
+++ b/solution.py
@@ -43,7 +43,7 @@
 def kernel(
     g, lf, lr, rq, rkv, rqr, rkvr, mom,
     gathered, scale_row, left_new, rq_new, rkv_new, mom_new,
-    own, sib, part, recv1, acc, part2, recv2, total,
+    own, sib, part, recv1, acc, shares, total,
     lf_v, lr_v, rq_v, rkv_v, rqr_v, rkvr_v, mom_v,
     roots_by, diag, slab, norm, norm_in,
     ssem, rsem, lsem, known,
@@ -190,59 +190,57 @@
     odd_u = [lax.rem(u[h], 2) for h in halves]
     odd_v = [lax.rem(v[h], 2) for h in halves]
 
-    def quad_sum(h, flip_u, flip_v):
-        a = 1 - odd_u[h] if flip_u else odd_u[h]
-        b = 1 - odd_v[h] if flip_v else odd_v[h]
-        value = acc[h, a, b]
+    corners = [(a, b) for a in range(2) for b in range(2)]
+    for h in halves:
+        place = 2 * odd_u[h] + odd_v[h]
+        all_of(recv1.at[h], incoming=("step1", h))
+        for a, b in corners:
+            value = acc[h, a, b]
+            for i in range(3):
+                value = value + recv1[h, i, a, b].astype(f32)
+            shares[h, place, a, b] = value.astype(bf16)
+        mine_share = shares.at[h, place]
         for i in range(3):
-            value = value + recv1[h, i, a, b].astype(f32)
-        return value
-
-    kept = []
-    for h in halves:
-        all_of(recv1.at[h], incoming=("step1", h))
-        for i in range(3):
-            part2[h, i] = quad_sum(h, *FLIPS[i]).astype(bf16)
-            send(part2.at[h, i], recv2.at[h, i], small[h][i], "step2", ("step2", h))
-        kept.append(quad_sum(h, 0, 0))
-    three = recv2.at[0]
+            send(mine_share, mine_share, small[h][i], "step2", ("step2", h))
+    three = recv1.at[0, :, 0, 0]
 
     def across(ref, name, h):
         block = ref.at[h, u[h], v[h], core]
         for i in range(3):
             send(block, block, small[h][i], "across" + name, ("across" + name, h))
 
-    for h in halves:
-        value = kept[h]
-        all_of(recv2.at[h], incoming=("step2", h))
-        for i in range(3):
-            value = value + recv2[h, i].astype(f32)
-        total[h, u[h], v[h], core] = value.astype(bf16)
-        across(total, "0", h)
-
     def group(ref, h, flip_u, flip_v):
         i = 1 - pair_u[h] if flip_u else pair_u[h]
         j = 1 - pair_v[h] if flip_v else pair_v[h]
         return ref.at[h, pl.ds(2 * i, 2), pl.ds(2 * j, 2), core]
 
-    def gather(ref, name, early, middle, late):
-        early()
-        for h in halves:
-            all_of(three, incoming=("across" + name, h))
-            block = group(ref, h, 0, 0)
-            for i in range(3):
-                send(block, block, large[h][i], "along" + name, ("along" + name, h, i))
-        for h in halves:
-            block = group(ref, h, 0, 0)
-            send(block, block, sibling, "over" + name, "over" + name)
-        middle()
+    def spread(ref, name, h):
+        block = group(ref, h, 0, 0)
+        for i in range(3):
+            send(block, block, large[h][i], "along" + name, ("along" + name, h, i))
+
+    def hand_over(ref, name, h, flips):
+        block = group(ref, h, *flips)
+        send(block, block, sibling, "over" + name, "over" + name)
+
+    def collect(ref, name, late):
         for i in (1, 2, 0):
             for h in halves:
-                block = group(ref, h, *FLIPS[i])
-                all_of(block, incoming=("along" + name, h, i))
-                send(block, block, sibling, "over" + name, "over" + name)
+                all_of(group(ref, h, *FLIPS[i]), incoming=("along" + name, h, i))
+                hand_over(ref, name, h, FLIPS[i])
         late()
         all_of(ref.at[:, :, :, other], incoming="over" + name)
+
+    for h in halves:
+        all_of(shares.at[h, 0:3], incoming=("step2", h))
+        for a, b in corners:
+            value = shares[h, 0, a, b].astype(f32)
+            for i in range(1, 4):
+                value = value + shares[h, i, a, b].astype(f32)
+            total[h, 2 * pair_u[h] + a, 2 * pair_v[h] + b, core] = value.astype(bf16)
+        spread(total, "0", h)
+    for h in halves:
+        hand_over(total, "0", h, (0, 0))
 
     lane = lax.broadcasted_iota(jnp.int32, (1, 2 * KC), 1)
     is_key = lane < KC
@@ -289,12 +287,11 @@
             copy.wait()
         saved.append(project(0, core))
 
-    def middle_part():
-        diagonal_part()
-        learn(1)
-        tell(2)
-
-    gather(total, "0", graft_part, middle_part, wait_loads)
+    learn(1)
+    tell(2)
+    graft_part()
+    diagonal_part()
+    collect(total, "0", wait_loads)
 
     def query_grad():
         return in_order(total, slice(0, QC))
@@ -368,15 +365,16 @@
         moved = pltpu.roll(square, KC, 1)
         rkv_new[1] = factor_keep * rkv_v[1] + factor_add * moved[KC:, :KC]
 
-    def early_part():
-        left_part()
-        norm_step(1)
-        right_part()
-        learn(2)
-        norm_step(2)
-
-    def wait_rest():
-        pass
+    left_part()
+    norm_step(1)
+    for h in halves:
+        all_of(three, incoming=("across1", h))
+        spread(gathered, "1", h)
+    for h in halves:
+        hand_over(gathered, "1", h, (0, 0))
+    right_part()
+    learn(2)
+    norm_step(2)
 
     def scale_part():
         sums = norm_add(2)
@@ -396,13 +394,13 @@
         scale_row[:, :QC] = jnp.broadcast_to(scale_q, (8, QC))
         scale_row[:, QC:] = jnp.broadcast_to(jnp.where(is_key, scale_k, scale_v), (8, 2 * KC))
 
-    gather(gathered, "1", early_part, wait_rest, scale_part)
+    collect(gathered, "1", scale_part)
 
     all_of(sib, outgoing="pair")
     all_of(recv1, outgoing="step1")
-    all_of(recv2, outgoing="step2")
+    all_of(recv1, outgoing="step2")
+    all_of(recv1.at[:, :, 0, 0], outgoing="across1")
     for name, ref in (("0", total), ("1", gathered)):
-        all_of(recv2, outgoing="across" + name)
         all_of(recv1, outgoing="along" + name)
         all_of(ref.at[:, :, :, core], outgoing="over" + name)
     all_of(norm_in.at[: 7 + 3 + depth - 1], outgoing="norm")
@@ -455,8 +453,7 @@
             pltpu.VMEM((2, 3) + quad_block, bf16),
             pltpu.VMEM((2, 3) + quad_block, bf16),
             pltpu.VMEM((2,) + quad_block, f32),
-            pltpu.VMEM((2, SIDE - 1, HALF, COLS), bf16),
-            pltpu.VMEM((2, SIDE - 1, HALF, COLS), bf16),
+            pltpu.VMEM((2, 4) + quad_block, bf16),
             pltpu.VMEM(by_half, bf16),
             pltpu.VMEM((3, PANEL, ORDER), f32),
             pltpu.VMEM((3, PANEL, ORDER), bf16),
@@ -470,8 +467,8 @@
             pltpu.VMEM((128, QC), f32),
             pltpu.VMEM((3, 8, 128), f32),
             pltpu.VMEM((12 + depth, 8, 128), f32),
-            pltpu.SemaphoreType.DMA((10,)),
-            pltpu.SemaphoreType.DMA((33,)),
+            pltpu.SemaphoreType.DMA((9,)),
+            pltpu.SemaphoreType.DMA((31,)),
             pltpu.SemaphoreType.DMA((15,)),
             pltpu.SemaphoreType.REGULAR((3,)),
         ],

time: 52 us -> 51.5 us (level)
  Pallas kernels: 51.2 us -> 50.5 us
    pallas_call x1, Pallas kernels: 49.9 us -> 49.2 us  [local_step(): pl.pallas_call(kernel, out_shape=(shape(by_half, bf16), shape((8, COLS),...]
where the time goes in v7:
time: 51.5 us; the launch traced here: 51.2 us
  Pallas kernels  50.5 us (98%)
  between operations  0.64 us (1%)
    pallas_call x1, Pallas kernels, local_step(): pl.pallas_call(kernel, out_shape=(shape(by_half, bf16), shape((8, COLS),...  49.2 us
    pallas_call x1, Pallas kernels, local_step(): pl.pallas_call(finish, out_shape=(shape((ORDER, COLS), bf16), shape((3, P...  1.31 us

profile of v7, /device:TPU:1, one launch (start us, length us, event | category | flops | bytes accessed | tf_op | source)
XLA Modules:
  0.0 51.2 jit_solution(9572394295493913597)
XLA Ops:
  0.6 49.2 %shard_map.119 = (bf16[2,4,4,2,16,640]{5,4,3,2,1,0:T(8,128)(2,1)S(1)}, f32[8,640]{1,0:T(8,128)S(1)}, f32[3,32,1024]{2,1,0:T(8,128)S(1)}, f32[16,512]{1,0:T(8,128...) custom-call(bf16[4,4,2,2,16,640]{5,4,3,2,1,0:T(8,128)(2,1)} %bitcast.10, f32[3,32,1024]{2,1,0:T(8,128)} %bitcast.12, ...), custom_call_target="tpu_custom_call" | custom-call | tf_op jit(solution)/shard_map/pallas_call | solution.py:438
  49.8 1.3 %shard_map.120 = (bf16[1024,640]{1,0:T(8,128)(2,1)}, f32[3,32,1024]{2,1,0:T(8,128)}, f32[16,512]{1,0:T(8,128)}, f32[2,64,64]{2,1,0:T(8,128)}, f32[32,640]{1,0:T(8,128)}) custom-call(bf16[2,4,4,2,16,640]{5,4,3,2,1,0:T(8,128)(2,1)S(1)} %get-tuple-element.16.gathered, f32[8,640]{1,0:T(8,128)S(1)} %get-tuple-element.17.scale_row, ...), custom_call_target="tpu_custom_call" | custom-call | tf_op jit(solution)/shard_map/pallas_call | solution.py:487

commit v8 on v7

--- a/solution.py
+++ b/solution.py
@@ -245,12 +245,17 @@
     lane = lax.broadcasted_iota(jnp.int32, (1, 2 * KC), 1)
     is_key = lane < KC
 
-    def to_lanes(square):
+    def as_row(square, start):
         column = jnp.sum(square, axis=0, keepdims=True)
         query = column[:, :128]
         for i in range(1, QC // 128):
             query = query + column[:, 128 * i : 128 * (i + 1)]
-        return query, column[:, QC:]
+        tail = column[:, QC:]
+        parts = (query, jnp.where(is_key, tail, 0.0), jnp.where(is_key, 0.0, tail))
+        row = jnp.zeros((1, 128), f32)
+        for i in range(3):
+            row = jnp.where(lane == start + i, jnp.sum(parts[i], axis=1, keepdims=True), row)
+        return row
 
     def my_rows():
         return jnp.concatenate([total[h, u[h], v[h], core] for h in halves], axis=0)
@@ -261,10 +266,7 @@
         moment_new = moment_keep * mom_v[...] + moment_add * row_grad * row_grad
         mom_new[...] = moment_new
         graft = row_grad / (jnp.sqrt(moment_new) + graft_eps)
-        graft_q, graft_kv = to_lanes(jnp.square(graft))
-        norm[0] = jnp.zeros((8, 128), f32)
-        norm[0, 0:1, :] = graft_q
-        norm[0, 1:2, :] = graft_kv
+        norm[0] = as_row(jnp.square(graft), 0)
 
     def diagonal_part():
         rkvr_load.wait()
@@ -331,9 +333,7 @@
         norm_send(level)
 
     square = jnp.square(jnp.concatenate([cond_q, cond_kv], axis=1))
-    cond_lanes_q, cond_lanes_kv = to_lanes(square)
-    norm[0, 2:3, :] = cond_lanes_q
-    norm[0, 3:4, :] = cond_lanes_kv
+    norm[0] = norm[0] + as_row(square, 3)
     norm_send(0)
     for h in halves:
         rows = slice(HALF * h, HALF * (h + 1))
@@ -370,27 +370,19 @@
     for h in halves:
         all_of(three, incoming=("across1", h))
         spread(gathered, "1", h)
+    learn(2)
+    norm_step(2)
     for h in halves:
         hand_over(gathered, "1", h, (0, 0))
     right_part()
-    learn(2)
-    norm_step(2)
 
     def scale_part():
         sums = norm_add(2)
 
-        def whole(row_index, mask):
-            values = sums[row_index : row_index + 1, :]
-            if mask is not None:
-                values = jnp.where(mask, values, 0.0)
-            return jnp.sum(values, axis=1, keepdims=True)
-
-        def scale(graft_sq, shampoo_sq):
-            return jnp.sqrt(graft_sq / (shampoo_sq + norm_eps))
-
-        scale_q = scale(whole(0, None), whole(2, None))
-        scale_k = scale(whole(1, is_key), whole(3, is_key))
-        scale_v = scale(whole(1, lane >= KC), whole(3, lane >= KC))
+        scales = jnp.sqrt(sums / (pltpu.roll(sums, 125, 1) + norm_eps))
+        scale_q, scale_k, scale_v = (
+            jnp.sum(jnp.where(lane == i, scales, 0.0), axis=1, keepdims=True) for i in range(3)
+        )
         scale_row[:, :QC] = jnp.broadcast_to(scale_q, (8, QC))
         scale_row[:, QC:] = jnp.broadcast_to(jnp.where(is_key, scale_k, scale_v), (8, 2 * KC))
 
@@ -465,8 +457,8 @@
             pltpu.VMEM((2, 3 * PANEL, ORDER // 2), bf16),
             pltpu.VMEM((2 * KC, 2 * KC), bf16),
             pltpu.VMEM((128, QC), f32),
-            pltpu.VMEM((3, 8, 128), f32),
-            pltpu.VMEM((12 + depth, 8, 128), f32),
+            pltpu.VMEM((3, 1, 128), f32),
+            pltpu.VMEM((12 + depth, 1, 128), f32),
             pltpu.SemaphoreType.DMA((9,)),
             pltpu.SemaphoreType.DMA((31,)),
             pltpu.SemaphoreType.DMA((15,)),

time: 51.5 us -> 50.9 us (0.988)
    pallas_call x1, Pallas kernels: 49.2 us -> 48.7 us  [local_step(): pl.pallas_call(kernel, out_shape=(shape(by_half, bf16), shape((8, COLS),...]
where the time goes in v8:
time: 50.9 us; the launch traced here: 50.6 us
  Pallas kernels  50 us (98%)
  between operations  0.64 us (1%)
    pallas_call x1, Pallas kernels, local_step(): pl.pallas_call(kernel, out_shape=(shape(by_half, bf16), shape((8, COLS),...  48.7 us
    pallas_call x1, Pallas kernels, local_step(): pl.pallas_call(finish, out_shape=(shape((ORDER, COLS), bf16), shape((3, P...  1.31 us

profile of v8, /device:TPU:1, one launch (start us, length us, event | category | flops | bytes accessed | tf_op | source)
XLA Modules:
  0.0 50.6 jit_solution(7224539661948100836)
XLA Ops:
  0.6 48.7 %shard_map.119 = (bf16[2,4,4,2,16,640]{5,4,3,2,1,0:T(8,128)(2,1)S(1)}, f32[8,640]{1,0:T(8,128)S(1)}, f32[3,32,1024]{2,1,0:T(8,128)S(1)}, f32[16,512]{1,0:T(8,128...) custom-call(bf16[4,4,2,2,16,640]{5,4,3,2,1,0:T(8,128)(2,1)} %bitcast.10, f32[3,32,1024]{2,1,0:T(8,128)} %bitcast.12, ...), custom_call_target="tpu_custom_call" | custom-call | tf_op jit(solution)/shard_map/pallas_call | solution.py:430
  49.3 1.3 %shard_map.120 = (bf16[1024,640]{1,0:T(8,128)(2,1)}, f32[3,32,1024]{2,1,0:T(8,128)}, f32[16,512]{1,0:T(8,128)}, f32[2,64,64]{2,1,0:T(8,128)}, f32[32,640]{1,0:T(8,128)}) custom-call(bf16[2,4,4,2,16,640]{5,4,3,2,1,0:T(8,128)(2,1)S(1)} %get-tuple-element.16.gathered, f32[8,640]{1,0:T(8,128)S(1)} %get-tuple-element.17.scale_row, ...), custom_call_target="tpu_custom_call" | custom-call | tf_op jit(solution)/shard_map/pallas_call | solution.py:479

commit v9 on v8

--- a/solution.py
+++ b/solution.py
@@ -365,11 +365,11 @@
         moved = pltpu.roll(square, KC, 1)
         rkv_new[1] = factor_keep * rkv_v[1] + factor_add * moved[KC:, :KC]
 
-    left_part()
-    norm_step(1)
     for h in halves:
         all_of(three, incoming=("across1", h))
         spread(gathered, "1", h)
+    norm_step(1)
+    left_part()
     learn(2)
     norm_step(2)
     for h in halves:

time: 50.9 us -> 54.8 us (1.077)
  Pallas kernels: 50 us -> 54.1 us
    pallas_call x1, Pallas kernels: 48.7 us -> 52.7 us  [local_step(): pl.pallas_call(kernel, out_shape=(shape(by_half, bf16), shape((8, COLS),...]
where the time goes in v9:
time: 54.8 us; the launch traced here: 54.7 us
  Pallas kernels  54.1 us (99%)
  between operations  0.64 us (1%)
    pallas_call x1, Pallas kernels, local_step(): pl.pallas_call(kernel, out_shape=(shape(by_half, bf16), shape((8, COLS),...  52.7 us
    pallas_call x1, Pallas kernels, local_step(): pl.pallas_call(finish, out_shape=(shape((ORDER, COLS), bf16), shape((3, P...  1.31 us

profile of v9, /device:TPU:1, one launch (start us, length us, event | category | flops | bytes accessed | tf_op | source)
XLA Modules:
  0.0 54.7 jit_solution(3187964079432926015)
XLA Ops:
  0.6 52.7 %shard_map.119 = (bf16[2,4,4,2,16,640]{5,4,3,2,1,0:T(8,128)(2,1)S(1)}, f32[8,640]{1,0:T(8,128)S(1)}, f32[3,32,1024]{2,1,0:T(8,128)S(1)}, f32[16,512]{1,0:T(8,128...) custom-call(bf16[4,4,2,2,16,640]{5,4,3,2,1,0:T(8,128)(2,1)} %bitcast.10, f32[3,32,1024]{2,1,0:T(8,128)} %bitcast.12, ...), custom_call_target="tpu_custom_call" | custom-call | tf_op jit(solution)/shard_map/pallas_call | solution.py:430
  53.4 1.3 %shard_map.120 = (bf16[1024,640]{1,0:T(8,128)(2,1)}, f32[3,32,1024]{2,1,0:T(8,128)}, f32[16,512]{1,0:T(8,128)}, f32[2,64,64]{2,1,0:T(8,128)}, f32[32,640]{1,0:T(8,128)}) custom-call(bf16[2,4,4,2,16,640]{5,4,3,2,1,0:T(8,128)(2,1)S(1)} %get-tuple-element.16.gathered, f32[8,640]{1,0:T(8,128)S(1)} %get-tuple-element.17.scale_row, ...), custom_call_target="tpu_custom_call" | custom-call | tf_op jit(solution)/shard_map/pallas_call | solution.py:479
